TPU v7x, 32 devices: a whole 2x2x4 slice. The times are simulated.
32 devices in a mesh: gx: 4 (over x, core), yz: 8 (over z, y).
Axes of the slice: x: 2, y: 2, z: 4, core: 2. Of those that a mesh axis runs over, the one named last changes fastest.
Arguments:
- displacement: float32 [3, 32, 128, 2048], P(None, 'gx', 'yz'), may hold values from -1.2 to 1.2
- force: float32 [3, 32, 128, 2048], P(None, 'gx', 'yz'), may hold values from -1.2 to 1.2
- damage: float32 [32, 128, 2048], P('gx', 'yz'), may hold values from 0 to 0.6
- history_old: float32 [32, 128, 2048], P('gx', 'yz'), may hold values from 0 to 0.5
- material: int32 [32, 128, 2048], P('gx', 'yz'), may hold values from 0 to 3
- patch_ids: int32 [32, 12], P(('gx', 'yz')), may hold values from 0 to 15, as said below
- owners: int32 [32, 12, 1], P(('gx', 'yz')), may hold values from 0 to 7; in each aligned block of 12 rows (0 to 11, 12 to 23, ..., all dimensions but the last counted through in order) at most 2 rows name the same one
- toughness: float32 [32, 8, 2, 8, 16, 128], P(('gx', 'yz')), may hold values from 0.5 to 2
Outputs:
- new_displacement: float32 [3, 32, 128, 2048], P(None, 'gx', 'yz')
- history: float32 [32, 128, 2048], P('gx', 'yz')
- new_damage: float32 [32, 128, 2048], P('gx', 'yz')
Inputs may be any that keep to these rules, and one draw needn't show every extreme that they name: `owners`: the entries of one device name one owner at most 2 times, and exactly 2 times in some devices. `patch_ids`: the 12 entries of one device are distinct.
All inputs are finite; a program needn't handle non-finite values.
Results may differ from a plain program's by a relative error of at most 0.0001.
Values sent between devices are 32-bit elements; how exact they have to be, the bound alone decides.
No kernel may reach another device: no remote copies, remote signals or barrier semaphores. Data moves between devices by JAX's collectives and lax.ppermute only.
A program may use at most 128 MiB of HBM per device.

v0:
```python
import jax
import jax.numpy as jnp
from jax import lax
from jax.experimental import pallas as pl
from jax.experimental.pallas import tpu as pltpu
from jax.sharding import PartitionSpec as P

SWEEPS = 8
MODULI = (1.0, 0.5, 4.0, 0.25)
SPRING = 0.05
RELAX = 0.8
LENGTH = 2.0
ROWS = 8
LANES = 128
LOW, HIGH = 0, 1
GRANT = 8 * 1024 * 1024

VMEM = pltpu.MemorySpace.VMEM
HBM = pltpu.MemorySpace.HBM
F32 = jnp.float32


def modulus(material):
    low = jnp.where(material == 0, MODULI[0], MODULI[1])
    high = jnp.where(material == 2, MODULI[2], MODULI[3])
    return jnp.where(material < 2, low, high)


def lane_index():
    return lax.broadcasted_iota(jnp.int32, (ROWS, LANES), 1)


def row_index():
    return lax.broadcasted_iota(jnp.int32, (ROWS, LANES), 0)


def where_tile(lead, t, k):
    return (*lead, slice(t * ROWS, (t + 1) * ROWS), slice(k * LANES, (k + 1) * LANES))


def tile(ref, lead, t, k):
    return ref[where_tile(lead, t, k)]


def put(ref, lead, t, k, value):
    ref[where_tile(lead, t, k)] = value


def moved(value, source, target):
    shift = (target - source) % ROWS if isinstance(source, int) else (target - source + ROWS) % ROWS
    if isinstance(shift, int) and shift == 0:
        return value
    return pltpu.roll(value, shift, 0)


class Line:
    def __init__(self, load, nk):
        self.load, self.nk, self.kept = load, nk, {}

    def get(self, kind, k):
        k = k % self.nk
        if (kind, k) not in self.kept:
            if kind == "own":
                value = self.load(k)
            else:
                value = pltpu.roll(self.get("own", k), LANES - 1 if kind == "next" else 1, 1)
            self.kept[kind, k] = value
        return self.kept[kind, k]

    def own(self, k):
        return self.get("own", k)

    def after(self, k):
        return jnp.where(lane_index() == LANES - 1, self.get("next", k + 1), self.get("next", k))

    def before(self, k):
        return jnp.where(lane_index() == 0, self.get("prev", k - 1), self.get("prev", k))


def y_before(column):
    rolled = [pltpu.roll(v, 1, 0) for v in column]
    row = row_index()
    return rolled[:1] + [jnp.where(row == 0, a, b) for a, b in zip(rolled, rolled[1:])]


def y_after(column):
    rolled = [pltpu.roll(v, ROWS - 1, 0) for v in column]
    row = row_index()
    return [jnp.where(row == ROWS - 1, b, a) for a, b in zip(rolled, rolled[1:])] + rolled[-1:]


def by_parity(parity, even, odd, then):
    @pl.when(parity == 0)
    def _():
        then(odd, even)

    @pl.when(parity == 1)
    def _():
        then(even, odd)


class Halo:
    def __init__(self, axis, even, odd):
        place, size = lax.axis_index(axis), lax.axis_size(axis)
        self.even, self.odd = even, odd
        self.parity = place % 2
        self.inside = (place > 0, place < size - 1)

    def get(self, side, load):
        even, odd = load(self.even), load(self.odd)
        here = self.parity == (1 if side == LOW else 0)
        return jnp.where(self.inside[side], jnp.where(here, even, odd), 0.0)


def planes_of(nx, body):
    body(0, -1)

    def inner(x, _):
        body(x, 0)
        return 0

    lax.fori_loop(1, nx - 1, inner, 0)
    body(nx - 1, 1)


def start_all(copies):
    for copy in copies:
        copy.start()


def pack_planes(even, odd, read, nx, nt):
    def planes(low, high):
        for side, out in ((0, low), (nx - 1, high)):
            for t in range(nt):
                for c in range(out.shape[0]):
                    out[c, t * ROWS : (t + 1) * ROWS, :] = read(c, side, t)

    by_parity(lax.axis_index("gx") % 2, even, odd, planes)


def begin_kernel(damage, material, field, u, stiff, ye, yo, xe, xo, damage_kept, material_kept, sems):
    nx, ny, nz = stiff.shape
    nt = ny // ROWS
    copies = [
        pltpu.make_async_copy(damage, damage_kept, sems.at[0]),
        pltpu.make_async_copy(material, material_kept, sems.at[1]),
        pltpu.make_async_copy(field, u, sems.at[2]),
    ]
    start_all(copies)
    copies[0].wait()
    copies[1].wait()

    def plane(x, _):
        d = 1.0 - damage_kept[x]
        stiff[x] = modulus(material_kept[x]) * (d * d + 0.001)
        return 0

    lax.fori_loop(0, nx, plane, 0)
    copies[2].wait()

    def rows(low, high):
        for side, out in ((0, low), (ny - 1, high)):
            for x in range(nx):
                for c in range(3):
                    out[c, x : x + 1, :] = u[c, x, side : side + 1, :]
                out[3, x : x + 1, :] = stiff[x, side : side + 1, :]

    by_parity(lax.axis_index("yz") % 2, ye, yo, rows)

    def read(c, x, t):
        part = slice(t * ROWS, (t + 1) * ROWS)
        return u[c, x, part, :] if c < 3 else stiff[x, part, :]

    pack_planes(xe, xo, read, nx, nt)


def relax_inner(x, place, u, load, weights, scale, out, acc_x, acc_y, faces):
    nt, nk = u.shape[2] // ROWS, u.shape[3] // LANES
    lines = {(c, t): Line(lambda k, c=c, t=t: tile(u, (c, x), t, k), nk) for c in range(3) for t in range(nt)}
    for k in range(nk):
        found = [weights(x, t, k) for t in range(nt)]
        scales = [scale(x, t, k) for t in range(nt)]
        for c in range(3):
            column = [lines[c, t].own(k) for t in range(nt)]
            yb, ya = y_before(column), y_after(column)
            for t in range(nt):
                xh, xl, wya, wyb, wza, wzb = found[t]
                total = load(c, x, t, k)
                if place != 1:
                    total = total + xh * tile(u, (c, x + 1), t, k)
                if place != -1:
                    total = total + xl * tile(u, (c, x - 1), t, k)
                total = total + (wya * ya[t] + wyb * yb[t])
                total = total + (wza * lines[c, t].after(k) + wzb * lines[c, t].before(k))
                if place == -1:
                    put(acc_x, (LOW, c), t, k, total)
                if place == 1:
                    put(acc_x, (HIGH, c), t, k, total)
                if t == 0:
                    put(faces, (LOW, c, x), 0, k, total)
                if t == nt - 1:
                    put(faces, (HIGH, c, x), 0, k, total)
                put(out, (c, x), t, k, (1.0 - RELAX) * column[t] + scales[t] * total)


def compact_rows(faces, out, nx):
    for c in range(out.shape[1]):
        for x in range(nx):
            out[LOW, c, x : x + 1, :] = faces[LOW, c, x, 0:1, :]
            out[HIGH, c, x : x + 1, :] = faces[HIGH, c, x, ROWS - 1 : ROWS, :]


def inner_one_kernel(
    u, stiff, force, wx, wya, wyb, wza, wzb, scale, out, acc_x, acc_y, diag_x, diag_y, faces, diag_faces
):
    nx, ny, nz = stiff.shape
    nt, nk = ny // ROWS, nz // LANES

    def prepare(x, place):
        lane, row = lane_index(), row_index()
        lines = [Line(lambda k, t=t: tile(stiff, (x,), t, k), nk) for t in range(nt)]
        for k in range(nk):
            column = [lines[t].own(k) for t in range(nt)]
            yb, ya = y_before(column), y_after(column)
            for t in range(nt):
                s = column[t]
                half = 0.5 * s
                diag = SPRING * s
                if place != 1:
                    w = half + 0.5 * tile(stiff, (x + 1,), t, k)
                    put(wx, (x,), t, k, w)
                    diag = diag + w
                if place != -1:
                    diag = diag + (half + 0.5 * tile(stiff, (x - 1,), t, k))
                w = half + 0.5 * ya[t]
                if t == nt - 1:
                    w = jnp.where(row == ROWS - 1, 0.0, w)
                put(wya, (x,), t, k, w)
                diag = diag + w
                w = half + 0.5 * yb[t]
                if t == 0:
                    w = jnp.where(row == 0, 0.0, w)
                put(wyb, (x,), t, k, w)
                diag = diag + w
                w = half + 0.5 * lines[t].after(k)
                if k == nk - 1:
                    diag = diag + jnp.where(lane == LANES - 1, half, w)
                    w = jnp.where(lane == LANES - 1, 0.0, w)
                else:
                    diag = diag + w
                put(wza, (x,), t, k, w)
                w = half + 0.5 * lines[t].before(k)
                if k == 0:
                    diag = diag + jnp.where(lane == 0, half, w)
                    w = jnp.where(lane == 0, 0.0, w)
                else:
                    diag = diag + w
                put(wzb, (x,), t, k, w)
                put(scale, (x,), t, k, RELAX / diag)
                if place == -1:
                    put(diag_x, (LOW,), t, k, diag)
                if place == 1:
                    put(diag_x, (HIGH,), t, k, diag)
                if t == 0:
                    put(diag_faces, (LOW, 0, x), 0, k, diag)
                if t == nt - 1:
                    put(diag_faces, (HIGH, 0, x), 0, k, diag)

    planes_of(nx, prepare)
    inner_pass(u, force, wx, wya, wyb, wza, wzb, scale, out, acc_x, acc_y, faces)
    compact_rows(diag_faces, diag_y, nx)


def inner_pass(u, force, wx, wya, wyb, wza, wzb, scale, out, acc_x, acc_y, faces):
    nx = u.shape[1]

    def body(x, place):
        def weights(x, t, k):
            high = None if place == 1 else tile(wx, (x,), t, k)
            low = None if place == -1 else tile(wx, (x - 1,), t, k)
            return (high, low) + tuple(tile(w, (x,), t, k) for w in (wya, wyb, wza, wzb))

        relax_inner(
            x, place, u, lambda c, x, t, k: tile(force, (c, x), t, k), weights, lambda x, t, k: tile(scale, (x,), t, k), out,
            acc_x, acc_y, faces,
        )

    planes_of(nx, body)
    compact_rows(faces, acc_y, nx)


def x_part(value, c, t, k):
    return tile(value[t], (c,), 0, k) if isinstance(value, tuple) else tile(value, (c,), t, k)


def own_side(parity, side, sent_even, sent_odd, lead, k):
    even, odd = tile(sent_even, lead, 0, k), tile(sent_odd, lead, 0, k)
    return jnp.where(parity == (1 if side == LOW else 0), even, odd)


def face_one_kernel(
    u, stiff, sye, syo, acc_x, acc_y, diag_x, diag_y, hye, hyo, hxe, hxo,
    ye, yo, xe, xo, w_x, w_xy, s_x, w_y, w_yx, s_y, planes,
):
    _, nx, ny, nz = u.shape
    nt, nk = ny // ROWS, nz // LANES
    hy = Halo("yz", hye, hyo)
    hx = Halo("gx", hxe, hxo)
    row = row_index()

    def x_halo(side, c, t, k):
        return hx.get(side, lambda value: x_part(value, c, t, k))

    def y_halo(side, c, k):
        return hy.get(side, lambda ref: tile(ref, (c,), 0, k))

    def y_faces(even, odd):
        for side, out in ((LOW, odd), (HIGH, even)):
            y_row, t = (0, 0) if side == LOW else (ROWS - 1, nt - 1)
            for k in range(nk):
                own = own_side(hy.parity, side, sye, syo, (3,), k)
                w = 0.5 * (own + y_halo(side, 3, k))
                low = moved(x_halo(LOW, 3, t, k), y_row, 0)
                high = moved(x_halo(HIGH, 3, t, k), y_row, ROWS - 1)
                edge = jnp.where(row == 0, low, high)
                we = jnp.where((row == 0) | (row == ROWS - 1), 0.5 * (own + edge), 0.0)
                scale = RELAX / (tile(diag_y, (side, 0), 0, k) + w + we)
                put(w_y, (side,), 0, k, w)
                put(w_yx, (side,), 0, k, we)
                put(s_y, (side,), 0, k, scale)
                for c in range(3):
                    low = moved(x_halo(LOW, c, t, k), y_row, 0)
                    high = moved(x_halo(HIGH, c, t, k), y_row, ROWS - 1)
                    edge = jnp.where(row == 0, low, high)
                    total = tile(acc_y, (side, c), 0, k) + w * y_halo(side, c, k) + we * edge
                    own_u = own_side(hy.parity, side, sye, syo, (c,), k)
                    put(out, (c,), 0, k, (1.0 - RELAX) * own_u + scale * total)

    by_parity(hy.parity, ye, yo, lambda low, high: y_faces(high, low))

    for side in (LOW, HIGH):
            x = 0 if side == LOW else nx - 1
            for k in range(nk):
                for t in range(nt):
                    own = tile(stiff, (x,), t, k)
                    w = 0.5 * (own + x_halo(side, 3, t, k))
                    diag = tile(diag_x, (side,), t, k) + w
                    edge_side = LOW if t == 0 else HIGH if t == nt - 1 else None
                    if edge_side is not None:
                        y_row = 0 if t == 0 else ROWS - 1
                        we = 0.5 * (own + moved(y_halo(edge_side, 3, k), x, y_row))
                        we = jnp.where(row == y_row, we, 0.0)
                        diag = diag + we
                        put(w_xy, (side,), t, k, we)
                    scale = RELAX / diag
                    put(w_x, (side,), t, k, w)
                    put(s_x, (side,), t, k, scale)
                    for c in range(3):
                        total = tile(acc_x, (side, c), t, k) + w * x_halo(side, c, t, k)
                        if edge_side is not None:
                            total = total + we * moved(y_halo(edge_side, c, k), x, y_row)
                        value = (1.0 - RELAX) * tile(u, (c, x), t, k) + scale * total
                        put(planes, (side, c), t, k, value)

    def read(c, x, t):
        return planes[LOW if x == 0 else HIGH, c, t * ROWS : (t + 1) * ROWS, :]

    pack_planes(xe, xo, read, nx, nt)


def insert_faces(u, x_face, y_face):
    _, nx, ny, nz = u.shape
    nt, nk = ny // ROWS, nz // LANES
    for side, x in ((LOW, 0), (HIGH, nx - 1)):
        for c in range(3):
            for t in range(nt):
                for k in range(nk):
                    put(u, (c, x), t, k, x_face(side, c, t, k))

    def inner(x, _):
        row = row_index()
        for side, t, place in ((LOW, 0, 0), (HIGH, nt - 1, ROWS - 1)):
            for c in range(3):
                for k in range(nk):
                    value = moved(y_face(side, c, k), x, place)
                    put(u, (c, x), t, k, jnp.where(row == place, value, tile(u, (c, x), t, k)))
        return 0

    lax.fori_loop(1, nx - 1, inner, 0)


def inner_two_kernel(
    u_in, scale, force, wx, wya, wyb, wza, wzb, sye, syo, planes,
    u, out, acc_x, acc_y, faces,
):
    hy = lax.axis_index("yz") % 2
    insert_faces(u, lambda side, c, t, k: tile(planes, (side, c), t, k), lambda side, c, k: own_side(hy, side, sye, syo, (c,), k))
    inner_pass(u, force, wx, wya, wyb, wza, wzb, scale, out, acc_x, acc_y, faces)


def face_two_kernel(
    u, sye, syo, acc_x, acc_y, w_x, w_xy, s_x, w_y, w_yx, s_y, hye, hyo, hxe, hxo,
    x_low0, x_low1, y_low, x_high, y_high,
):
    _, nx, ny, nz = u.shape
    nt, nk = ny // ROWS, nz // LANES
    hy = Halo("yz", hye, hyo)
    hx = Halo("gx", hxe, hxo)
    row = row_index()

    def x_halo(side, c, t, k):
        return hx.get(side, lambda value: x_part(value, c, t, k))

    def y_halo(side, c, k):
        return hy.get(side, lambda ref: tile(ref, (c,), 0, k))

    for side, out in ((LOW, y_low), (HIGH, y_high)):
        y_row, t = (0, 0) if side == LOW else (ROWS - 1, nt - 1)
        for k in range(nk):
            w, we, scale = (tile(ref, (side,), 0, k) for ref in (w_y, w_yx, s_y))
            for c in range(3):
                low = moved(x_halo(LOW, c, t, k), y_row, 0)
                high = moved(x_halo(HIGH, c, t, k), y_row, ROWS - 1)
                edge = jnp.where(row == 0, low, high)
                total = tile(acc_y, (side, c), 0, k) + w * y_halo(side, c, k) + we * edge
                own_u = own_side(hy.parity, side, sye, syo, (c,), k)
                put(out, (c,), 0, k, (1.0 - RELAX) * own_u + scale * total)
    for side in (LOW, HIGH):
        x = 0 if side == LOW else nx - 1
        for k in range(nk):
            for t in range(nt):
                w, scale = tile(w_x, (side,), t, k), tile(s_x, (side,), t, k)
                edge_side = LOW if t == 0 else HIGH if t == nt - 1 else None
                for c in range(3):
                    total = tile(acc_x, (side, c), t, k) + w * x_halo(side, c, t, k)
                    if edge_side is not None:
                        y_row = 0 if t == 0 else ROWS - 1
                        total = total + tile(w_xy, (side,), t, k) * moved(y_halo(edge_side, c, k), x, y_row)
                    value = (1.0 - RELAX) * tile(u, (c, x), t, k) + scale * total
                    if side == LOW:
                        put((x_low0, x_low1)[t], (c,), 0, k, value)
                    else:
                        put(x_high, (c,), t, k, value)


def energy_kernel(
    u_in, x_low0, x_low1, y_low, x_high, y_high, material, history_old,
    u, u_out, history, top, half_top, far, half_far, rows, half_rows, sems,
):
    _, nx, ny, nz = u.shape
    nt, nk = ny // ROWS, nz // LANES
    x_low = (x_low0, x_low1)
    insert_faces(
        u,
        lambda side, c, t, k: x_part((x_low, x_high)[side], c, t, k),
        lambda side, c, k: tile((y_low, y_high)[side], (c,), 0, k),
    )
    copies = [pltpu.make_async_copy(u.at[c], u_out.at[c], sems.at[c]) for c in range(3)]
    start_all(copies)

    def body(x, place):
        lane, row = lane_index(), row_index()
        lines = {(c, t): Line(lambda k, c=c, t=t: tile(u, (c, x), t, k), nk) for c in range(3) for t in range(nt)}
        for k in range(nk):
            sums = [None] * nt
            for c in range(3):
                column = [lines[c, t].own(k) for t in range(nt)]
                ya = y_after(column)
                for t in range(nt):
                    v = column[t]
                    b = ya[t] - v
                    if t == nt - 1:
                        b = jnp.where(row == ROWS - 1, 0.0, b)
                    after = lines[c, t].after(k)
                    if k == nk - 1:
                        after = jnp.where(lane == LANES - 1, 0.0, after)
                    d = after - v
                    total = b * b + d * d
                    if place != 1:
                        a = tile(u, (c, x + 1), t, k) - v
                        total = total + a * a
                    sums[t] = total if c == 0 else sums[t] + total
            for t in range(nt):
                half = 0.5 * modulus(tile(material, (x,), t, k))
                if t == nt - 1:
                    put(rows, (x,), 0, k, sums[t])
                    put(half_rows, (x,), 0, k, half)
                if place == 1:
                    put(far, (), t, k, sums[t])
                    put(half_far, (), t, k, half)
                put(history, (x,), t, k, jnp.maximum(tile(history_old, (x,), t, k), half * sums[t]))

    planes_of(nx, body)
    for x in range(nx):
        top[x : x + 1, :] = rows[x, ROWS - 1 : ROWS, :]
        half_top[x : x + 1, :] = half_rows[x, ROWS - 1 : ROWS, :]
    for copy in copies:
        copy.wait()


def last_kernel(
    ids, owners, history_in, top, half_top, far, half_far, x_high, y_high, hy, hx0, hx1, tough_from, damage_from,
    history, history_out, damage_out, energy, damage, tough, sems,
):
    nx, ny, nz = damage.shape
    nt, nk = ny // ROWS, nz // LANES
    count = ids.shape[1]
    hx = (hx0, hx1)
    fetched = [pltpu.make_async_copy(damage_from, damage, sems.at[2])]
    for n in range(count):
        owner = owners[0, n]
        slot = sum([(owners[0, m] == owner).astype(jnp.int32) for m in range(n)], jnp.int32(0))
        fetched.append(pltpu.make_async_copy(tough_from.at[owner, slot], tough.at[n], sems.at[3 + n]))
    start_all(fetched)

    def squares(here, beyond):
        return sum([(beyond(c) - here(c)) ** 2 for c in range(3)])

    for k in range(nk):
        total = tile(top, (), 0, k) + squares(lambda c: tile(y_high, (c,), 0, k), lambda c: tile(hy, (c,), 0, k))
        put(energy, (), 0, k, tile(half_top, (), 0, k) * total)

    def body(x, _):
        for k in range(nk):
            value = jnp.where(row_index() == ROWS - 1, moved(tile(energy, (), 0, k), x, ROWS - 1), 0.0)
            put(history, (x,), nt - 1, k, jnp.maximum(tile(history, (x,), nt - 1, k), value))
        return 0

    lax.fori_loop(0, nx - 1, body, 0)
    for k in range(nk):
        y_term = squares(lambda c: tile(y_high, (c,), 0, k), lambda c: tile(hy, (c,), 0, k))
        for t in range(nt):
            total = tile(far, (), t, k) + squares(lambda c: tile(x_high, (c,), t, k), lambda c: x_part(hx, c, t, k))
            if t == nt - 1:
                total = total + jnp.where(row_index() == ROWS - 1, moved(y_term, nx - 1, ROWS - 1), 0.0)
            put(history, (nx - 1,), t, k, jnp.maximum(tile(history, (nx - 1,), t, k), tile(half_far, (), t, k) * total))
    saved = pltpu.make_async_copy(history, history_out, sems.at[0])
    saved.start()
    for copy in fetched:
        copy.wait()
    per = max(n for n in (1, 2, 3, 4, 6) if count % n == 0)
    cells = [(x, t) for x in range(nx) for t in range(nt)]
    i = lax.broadcasted_iota(jnp.int32, (2 * LANES, LANES), 0) % LANES
    j = lax.broadcasted_iota(jnp.int32, (2 * LANES, LANES), 1)
    beside = (i - j == 1) | (j - i == 1) | ((i == j) & ((i == 0) | (i == LANES - 1)))
    beside = jnp.where(beside, 1.0, 0.0).astype(jnp.bfloat16)

    def z_sums(d):
        whole = jnp.concatenate([d[cell] for cell in cells], axis=0)
        main = whole.astype(jnp.bfloat16)
        rest = (whole - main.astype(F32)).astype(jnp.bfloat16)
        sums = jnp.dot(jnp.concatenate([main, rest], axis=1), beside, preferred_element_type=F32)
        return {cell: sums[n * ROWS : (n + 1) * ROWS] for n, cell in enumerate(cells)}

    def sweep(first, second, d):
        row = row_index()
        sums, new = z_sums(d), {}
        for x in range(nx):
            column = [d[x, t] for t in range(nt)]
            yb, ya = y_before(column), y_after(column)
            yb[0] = jnp.where(row == 0, column[0], yb[0])
            ya[-1] = jnp.where(row == ROWS - 1, column[-1], ya[-1])
            for t in range(nt):
                total = (d[min(x + 1, nx - 1), t] + d[max(x - 1, 0), t]) + (ya[t] + yb[t]) + sums[x, t]
                new[x, t] = first[x, t] + second[x, t] * total
        return new

    def group(q, _):
        states = []
        for p in range(per):
            n = q * per + p
            lanes = pl.ds(pl.multiple_of(ids[0, n] * LANES, LANES), LANES)
            first, second, d = {}, {}, {}
            for x, t in cells:
                part = slice(t * ROWS, (t + 1) * ROWS)
                h2 = 2.0 * history[x, part, lanes]
                g = tough[n, x, part, :]
                g2 = g * LENGTH
                inverse = 1.0 / (g / LENGTH + h2 + 6.0 * g2)
                first[x, t] = h2 * inverse
                second[x, t] = g2 * inverse
                d[x, t] = damage[x, part, lanes]
            states.append((lanes, first, second, d))
        for _ in range(SWEEPS):
            states = [(lanes, first, second, sweep(first, second, d)) for lanes, first, second, d in states]
        for lanes, _, _, d in states:
            for x, t in cells:
                part = slice(t * ROWS, (t + 1) * ROWS)
                damage[x, part, lanes] = jnp.maximum(d[x, t], damage[x, part, lanes])
        return 0

    lax.fori_loop(0, count // per, group, 0)
    done = pltpu.make_async_copy(damage, damage_out, sems.at[1])
    done.start()
    saved.wait()
    done.wait()


def even_pairs(axis):
    size = lax.axis_size(axis)
    pairs = [(i, i + 1) for i in range(0, size - 1, 2)]
    return pairs + [(b, a) for a, b in pairs]


def odd_pairs(axis):
    gx, yz = lax.axis_size("gx"), lax.axis_size("yz")

    def number(place, other):
        return place * yz + other if axis == "gx" else other * yz + place

    size, others = (gx, yz) if axis == "gx" else (yz, gx)
    step = 2 if axis == "gx" else 1
    pairs = [(number(i, o), number(i + 1, o)) for i in range(1, size - 1, 2) for o in range(others)]
    if size % 2 == 0 and others % (2 * step) == 0:
        for end in (0, size - 1):
            pairs += [(number(end, o), number(end, o + step)) for o in range(others) if o % (2 * step) < step]
    return pairs + [(b, a) for a, b in pairs]


def exchange(ye, yo, xe, xo):
    both = ("gx", "yz")
    return (
        lax.ppermute(ye, "yz", even_pairs("yz")),
        lax.ppermute(yo, both, odd_pairs("yz")),
        lax.ppermute(xe, "gx", even_pairs("gx")),
        lax.ppermute(xo, both, odd_pairs("gx")),
    )


def from_above(value, axis):
    size = lax.axis_size(axis)
    return lax.ppermute(value, axis, [(i + 1, i) for i in range(size - 1)])


def call(kernel, outs, ins, scratch=(), aliases=None):
    args, in_specs, out_specs, shapes = [], [], [], []
    for value, space in ins:
        args.append(value if space is pltpu.SMEM else pltpu.with_memory_space_constraint(value, space))
        in_specs.append(pl.BlockSpec(memory_space=space))
    for shape, space in outs:
        shapes.append(space(shape, F32))
        out_specs.append(pl.BlockSpec(memory_space=space))
    return pl.pallas_call(
        kernel,
        out_shape=shapes,
        in_specs=in_specs,
        out_specs=out_specs,
        scratch_shapes=scratch,
        input_output_aliases=aliases or {},
        compiler_params=pltpu.CompilerParams(vmem_limit_bytes=GRANT),
    )(*args)


def here(*shapes):
    return [(shape, VMEM) for shape in shapes]


def kept(*values):
    return [(value, VMEM) for value in values]


def far_off(*values):
    return [(value, HBM) for value in values]


def body(displacement, force, damage, history_old, material, patch_ids, owners, toughness):
    nx, ny, nz = damage.shape
    assert nx == ROWS and ny == 2 * ROWS
    full, cells, halves = (3, nx, ny, nz), (nx, ny, nz), (3, ROWS, nz)

    def faces(count):
        return here(*[(count, nx, nz)] * 2, *[(count, ny, nz)] * 2)

    def copies(count):
        return pltpu.SemaphoreType.DMA((count,))

    arrived = lax.all_to_all(toughness[0], "yz", split_axis=0, concat_axis=0, tiled=True)
    u, stiff, *sent = call(
        begin_kernel,
        here(full, cells) + faces(4),
        far_off(damage, material, displacement),
        [pltpu.VMEM(cells, F32), pltpu.VMEM(cells, jnp.int32), copies(3)],
    )
    brought = exchange(*sent)
    wx, wya, wyb, wza, wzb, scale, u1, acc_x, acc_y, diag_x, diag_y = call(
        inner_one_kernel,
        here((nx - 1, ny, nz), *[cells] * 5, full, (2, 3, ny, nz), (2, 3, nx, nz), (2, ny, nz), (2, 1, nx, nz)),
        kept(u, stiff, force),
        [pltpu.VMEM((2, 3, nx, ROWS, nz), F32), pltpu.VMEM((2, 1, nx, ROWS, nz), F32)],
    )
    *own, w_x, w_xy, s_x, w_y, w_yx, s_y, planes = call(
        face_one_kernel,
        faces(3) + here(*[(2, ny, nz)] * 3, *[(2, nx, nz)] * 3, (2, 3, ny, nz)),
        kept(u, stiff, sent[0], sent[1], acc_x, acc_y, diag_x, diag_y, *brought),
    )
    brought = exchange(*own)
    u1, u2, acc_x, acc_y = call(
        inner_two_kernel,
        here(full, full, (2, 3, ny, nz), (2, 3, nx, nz)),
        kept(u1, scale, force, wx, wya, wyb, wza, wzb, own[0], own[1], planes),
        [pltpu.VMEM((2, 3, nx, ROWS, nz), F32)],
        {0: 0},
    )
    x_low0, x_low1, y_low, x_high, y_high = call(
        face_two_kernel,
        here(halves, halves, (3, nx, nz), (3, ny, nz), (3, nx, nz)),
        kept(u1, own[0], own[1], acc_x, acc_y, w_x, w_xy, s_x, w_y, w_yx, s_y, *brought),
    )
    hy, hx0, hx1 = from_above(y_low, "yz"), from_above(x_low0, "gx"), from_above(x_low1, "gx")
    _, new_displacement, history, *sums = call(
        energy_kernel,
        here(full) + [(full, HBM)] + here(cells, *[(nx, nz)] * 2, *[(ny, nz)] * 2),
        kept(u2, x_low0, x_low1, y_low, x_high, y_high, material, history_old),
        [pltpu.VMEM((nx, ROWS, nz), F32), pltpu.VMEM((nx, ROWS, nz), F32), copies(3)],
        {0: 0},
    )
    count = patch_ids.shape[1]
    _, new_history, new_damage = call(
        last_kernel,
        here(cells) + [(cells, HBM), (cells, HBM)],
        [(patch_ids, pltpu.SMEM), (owners[:, :, 0], pltpu.SMEM)]
        + kept(history, *sums, x_high, y_high, hy, hx0, hx1)
        + far_off(arrived, damage),
        [pltpu.VMEM((nx, nz), F32), pltpu.VMEM(cells, F32), pltpu.VMEM((count,) + arrived.shape[2:], F32), copies(3 + count)],
        {2: 0},
    )
    return (new_displacement, new_history, new_damage)


def solution(mesh):
    return jax.shard_map(
        body,
        mesh=mesh,
        in_specs=(
            P(None, "gx", "yz", None),
            P(None, "gx", "yz", None),
            P("gx", "yz", None),
            P("gx", "yz", None),
            P("gx", "yz", None),
            P(("gx", "yz"), None),
            P(("gx", "yz"), None, None),
            P(("gx", "yz"), None, None, None, None, None),
        ),
        out_specs=(P(None, "gx", "yz", None), P("gx", "yz", None), P("gx", "yz", None)),
        check_vma=False,
    )
```

profile of v0, /device:TPU:9, one launch (start us, length us, event | category | flops | bytes accessed | tf_op | source)
XLA Modules:
  0.0 70.9 jit_solution(8084013834080174223)
XLA Ops:
  0.6 5.7 %all-to-all-start = ((f32[8,2,8,16,128]{4,3,2,1,0:T(8,128)}), f32[8,2,8,16,128]{4,3,2,1,0:T(8,128)}, u32[]{:S(2)}, u32[]{:S(2)}) async-start(f32[8,2,8,16,128]{4,3,2,1,0:T(8,128)} %bitcast.3), calls=%async_computation | async-start | bytes 2097152 | tf_op jit(solution)/shard_map/all_to_all | solution.py:677
  6.4 2.9 %shard_map.103 = (f32[3,8,16,2048]{3,2,1,0:T(8,128)S(1)}, f32[8,16,2048]{2,1,0:T(8,128)S(1)}, f32[4,8,2048]{2,1,0:T(8,128)S(1)}, f32[4,8,2048]{2,1,0:T(8,128)S(1...) custom-call(f32[8,16,2048]{2,1,0:T(8,128)} %damage_from.1, s32[8,16,2048]{2,1,0:T(8,128)} %material.3, ...), custom_call_target="tpu_custom_call" | custom-call | tf_op jit(solution)/shard_map/pallas_call | solution.py:643
  9.3 1.3 %collective-permute-start.2 = (f32[4,16,2048]{2,1,0:T(8,128)S(1)}, f32[4,16,2048]{2,1,0:T(8,128)S(1)}, u32[]{:S(2)}, u32[]{:S(2)}) collective-permute-start(f32[4,16,2048]{2,1,0:T(8,128)S(1)} %get-tuple-element.63), channel_id=1, source_target_pairs={{0,8},{16,24},{8,0},{24,16},{1,9},{17,25},{9,1},{25,17},{2,10},{18... | collective-permute-start | bytes 1572872 | tf_op jit(solution)/shard_map/ppermute | solution.py:625
  10.6 1.2 %collective-permute-start.3 = (f32[4,16,2048]{2,1,0:T(8,128)S(1)}, f32[4,16,2048]{2,1,0:T(8,128)S(1)}, u32[]{:S(2)}, u32[]{:S(2)}) collective-permute-start(f32[4,16,2048]{2,1,0:T(8,128)S(1)} %get-tuple-element.64), channel_id=1, source_target_pairs={{8,16},{9,17},{10,18},{11,19},{12,20},{13,21},{14,22},{15,23},{0,2... | collective-permute-start | bytes 1572872 | tf_op jit(solution)/shard_map/ppermute | solution.py:626
  11.8 1.2 %collective-permute-start = (f32[4,8,2048]{2,1,0:T(8,128)S(1)}, f32[4,8,2048]{2,1,0:T(8,128)S(1)}, u32[]{:S(2)}, u32[]{:S(2)}) collective-permute-start(f32[4,8,2048]{2,1,0:T(8,128)S(1)} %get-tuple-element.57.sye), channel_id=1, source_target_pairs={{0,1},{2,3},{4,5},{6,7},{1,0},{3,2},{5,4},{7,6},{8,9},{10,11},{12,... | collective-permute-start | bytes 786440 | tf_op jit(solution)/shard_map/ppermute | solution.py:623
  12.9 0.0 collective-permute-start.1
  13.0 3.8 %shard_map.104 = (f32[7,16,2048]{2,1,0:T(8,128)S(1)}, f32[8,16,2048]{2,1,0:T(8,128)S(1)}, f32[8,16,2048]{2,1,0:T(8,128)S(1)}, f32[8,16,2048]{2,1,0:T(8,128)S(1)}...) custom-call(f32[3,8,16,2048]{3,2,1,0:T(8,128)S(1)} %get-tuple-elemen, ...), custom_call_target="tpu_custom_call" | custom-call | tf_op jit(solution)/shard_map/pallas_call | solution.py:643
  16.8 6.9 %collective-permute-done.hye = f32[4,8,2048]{2,1,0:T(8,128)S(1)} collective-permute-done((f32[4,8,2048]{2,1,0:T(8,128)S(1)}, f32[4,8,2048]{2,1,0:T(8,128)S(1)}, u32[]{:S(2)}, u32[]{:S(2)}) %collective-permute-start) | collective-permute-done | bytes 262176 | tf_op jit(solution)/shard_map/ppermute | solution.py:623
  23.7 6.5 %collective-permute-done.1.hyo = f32[4,8,2048]{2,1,0:T(8,128)S(1)} collective-permute-done((f32[4,8,2048]{2,1,0:T(8,128)S(1)}, f32[4,8,2048]{2,1,0:T(8,128)S(1)}, u32[]{:S(2)}, u32[]{:S(2)}) %collective-permute-start.1) | collective-permute-done | bytes 262176 | tf_op jit(solution)/shard_map/ppermute | solution.py:624
  30.1 0.0 collective-permute-done.2.hxe
  30.1 0.8 %shard_map.105 = (f32[3,8,2048]{2,1,0:T(8,128)S(1)}, f32[3,8,2048]{2,1,0:T(8,128)S(1)}, f32[3,16,2048]{2,1,0:T(8,128)S(1)}, f32[3,16,2048]{2,1,0:T(8,128)S(1)}, ...) custom-call(f32[3,8,16,2048]{3,2,1,0:T(8,128)S(1)} %get-tuple-elemen, ...), custom_call_target="tpu_custom_call" | custom-call | tf_op jit(solution)/shard_map/pallas_call | solution.py:643
  30.9 7.4 %collective-permute-start.6 = (f32[3,16,2048]{2,1,0:T(8,128)S(1)}, f32[3,16,2048]{2,1,0:T(8,128)S(1)}, u32[]{:S(2)}, u32[]{:S(2)}) collective-permute-start(f32[3,16,2048]{2,1,0:T(8,128)S(1)} %get-tuple-element.78), channel_id=1, source_target_pairs={{0,8},{16,24},{8,0},{24,16},{1,9},{17,25},{9,1},{25,17},{2,10},{18... | collective-permute-start | bytes 1179656 | tf_op jit(solution)/shard_map/ppermute | solution.py:625
  38.4 0.9 %collective-permute-start.7 = (f32[3,16,2048]{2,1,0:T(8,128)S(1)}, f32[3,16,2048]{2,1,0:T(8,128)S(1)}, u32[]{:S(2)}, u32[]{:S(2)}) collective-permute-start(f32[3,16,2048]{2,1,0:T(8,128)S(1)} %get-tuple-element.79), channel_id=1, source_target_pairs={{8,16},{9,17},{10,18},{11,19},{12,20},{13,21},{14,22},{15,23},{0,2... | collective-permute-start | bytes 1179656 | tf_op jit(solution)/shard_map/ppermute | solution.py:626
  39.3 1.5 %collective-permute-start.4 = (f32[3,8,2048]{2,1,0:T(8,128)S(1)}, f32[3,8,2048]{2,1,0:T(8,128)S(1)}, u32[]{:S(2)}, u32[]{:S(2)}) collective-permute-start(f32[3,8,2048]{2,1,0:T(8,128)S(1)} %get-tuple-element.65.sye), channel_id=1, source_target_pairs={{0,1},{2,3},{4,5},{6,7},{1,0},{3,2},{5,4},{7,6},{8,9},{10,11},{12,... | collective-permute-start | bytes 589832 | tf_op jit(solution)/shard_map/ppermute | solution.py:623
  40.8 0.0 collective-permute-start.5
  40.8 3.0 %shard_map.106 = (f32[3,8,16,2048]{3,2,1,0:T(8,128)S(1)}, f32[3,8,16,2048]{3,2,1,0:T(8,128)S(1)}, f32[2,3,16,2048]{3,2,1,0:T(8,128)S(1)}, f32[2,3,8,2048]{3,2,1,0:T(8,128)S(1)}) custom-call(f32[3,8,16,2048]{3,2,1,0:T(8,128)S(1)} %get-tuple-element.50.u_in, f32[8,16,2048]{2,1,0:T(8,128)S(1)} %get-tuple-element.51.scale, ...), custom_call_target="tpu_custom_call", output_to_operand_aliasing={{0}: (0, {})} | custom-call | tf_op jit(solution)/shard_map/pallas_call | solution.py:643
  43.8 5.9 %collective-permute-done.4.hye = f32[3,8,2048]{2,1,0:T(8,128)S(1)} collective-permute-done((f32[3,8,2048]{2,1,0:T(8,128)S(1)}, f32[3,8,2048]{2,1,0:T(8,128)S(1)}, u32[]{:S(2)}, u32[]{:S(2)}) %collective-permute-start.4) | collective-permute-done | bytes 196640 | tf_op jit(solution)/shard_map/ppermute | solution.py:623
  49.7 0.0 collective-permute-done.7.hxo
  49.7 0.0 copy-start.1
  49.7 0.0 copy-start.2
  49.7 0.6 shard_map.107
  50.3 2.1 %collective-permute-start.8 = (f32[3,8,2048]{2,1,0:T(8,128)S(1)}, f32[3,8,2048]{2,1,0:T(8,128)S(1)}, u32[]{:S(2)}, u32[]{:S(2)}) collective-permute-start(f32[3,8,2048]{2,1,0:T(8,128)S(1)} %get-tuple-element.82.y_low), channel_id=1, source_target_pairs={{1,0},{2,1},{3,2},{4,3},{5,4},{6,5},{7,6},{9,8},{10,9},{11,10},{12... | collective-permute-start | bytes 589832 | tf_op jit(solution)/shard_map/ppermute | solution.py:632
  52.3 4.5 %collective-permute-start.9 = (f32[3,8,2048]{2,1,0:T(8,128)S(1)}, f32[3,8,2048]{2,1,0:T(8,128)S(1)}, u32[]{:S(2)}, u32[]{:S(2)}) collective-permute-start(f32[3,8,2048]{2,1,0:T(8,128)S(1)} %get-tuple-element.80.x_low0), channel_id=1, source_target_pairs={{8,0},{16,8},{24,16},{9,1},{17,9},{25,17},{10,2},{18,10},{26,18},{... | collective-permute-start | bytes 589832 | tf_op jit(solution)/shard_map/ppermute | solution.py:632
  56.9 1.9 %collective-permute-start.10 = (f32[3,8,2048]{2,1,0:T(8,128)S(1)}, f32[3,8,2048]{2,1,0:T(8,128)S(1)}, u32[]{:S(2)}, u32[]{:S(2)}) collective-permute-start(f32[3,8,2048]{2,1,0:T(8,128)S(1)} %get-tuple-element.81.x_low1), channel_id=1, source_target_pairs={{8,0},{16,8},{24,16},{9,1},{17,9},{25,17},{10,2},{18,10},{26,18},{... | collective-permute-start | bytes 589832 | tf_op jit(solution)/shard_map/ppermute | solution.py:632
  58.8 0.0 copy-start.3
  58.8 0.0 copy-start.4
  58.8 2.0 %shard_map.108 = (f32[3,8,16,2048]{3,2,1,0:T(8,128)S(1)}, f32[3,8,16,2048]{3,2,1,0:T(8,128)}, f32[8,16,2048]{2,1,0:T(8,128)S(1)}, f32[8,2048]{1,0:T(8,128)S(1)},...) custom-call(f32[3,8,16,2048]{3,2,1,0:T(8,128)S(1)} %get-tuple-elemen, ...), custom_call_target="tpu_custom_call", output_to_operand_aliasing={{0}: (0, {})} | custom-call | tf_op jit(solution)/shard_map/pallas_call | solution.py:643
  60.8 0.0 collective-permute-done.8.hy
  60.8 0.5 collective-permute-done.9.hx0
  61.4 2.5 %collective-permute-done.10.hx1 = f32[3,8,2048]{2,1,0:T(8,128)S(1)} collective-permute-done((f32[3,8,2048]{2,1,0:T(8,128)S(1)}, f32[3,8,2048]{2,1,0:T(8,128)S(1)}, u32[]{:S(2)}, u32[]{:S(2)}) %collective-permute-start.10) | collective-permute-done | bytes 196640 | tf_op jit(solution)/shard_map/ppermute | solution.py:632
  63.8 0.0 all-to-all-done.tough_from
  63.9 7.0 %shard_map.109 = (f32[8,16,2048]{2,1,0:T(8,128)S(1)}, f32[8,16,2048]{2,1,0:T(8,128)}, f32[8,16,2048]{2,1,0:T(8,128)}) custom-call(s32[1,12]{1,0:T(1,128)S(1)} %copy-done.3, s32[1,12]{1,0:T(1,128)S(1)} %bitcast.2, f32[8,16,2048]{2,1,0:T(8,128)S(1)} %get-tuple-element.86.history_in, ...), custom_call_target="tpu_custom_call", output_to_operand_aliasing={{0}: (2, {})} | custom-call | tf_op jit(solution)/shard_map/pallas_call | solution.py:643
  (9 shorter events, 0.0 us)
Async XLA Ops:
  0.6 63.2 %all-to-all-start = ((f32[8,2,8,16,128]{4,3,2,1,0:T(8,128)}), f32[8,2,8,16,128]{4,3,2,1,0:T(8,128)}, u32[]{:S(2)}, u32[]{:S(2)}) async-start(f32[8,2,8,16,128]{4,3,2,1,0:T(8,128)} %bitcast.3), calls=%async_computation | async-start | bytes 2097152 | tf_op jit(solution)/shard_map/all_to_all | solution.py:677
  6.4 6.6 %copy-start = (f32[3,8,16,2048]{3,2,1,0:T(8,128)S(1)}, f32[3,8,16,2048]{3,2,1,0:T(8,128)}, u32[]{:S(2)}) copy-start(f32[3,8,16,2048]{3,2,1,0:T(8,128)} %force.3) | copy-start | bytes 9437188
  9.3 20.9 %collective-permute-start.2 = (f32[4,16,2048]{2,1,0:T(8,128)S(1)}, f32[4,16,2048]{2,1,0:T(8,128)S(1)}, u32[]{:S(2)}, u32[]{:S(2)}) collective-permute-start(f32[4,16,2048]{2,1,0:T(8,128)S(1)} %get-tuple-element.63), channel_id=1, source_target_pairs={{0,8},{16,24},{8,0},{24,16},{1,9},{17,25},{9,1},{25,17},{2,10},{18... | collective-permute-start | bytes 1572872 | tf_op jit(solution)/shard_map/ppermute | solution.py:625
  10.6 19.6 %collective-permute-start.3 = (f32[4,16,2048]{2,1,0:T(8,128)S(1)}, f32[4,16,2048]{2,1,0:T(8,128)S(1)}, u32[]{:S(2)}, u32[]{:S(2)}) collective-permute-start(f32[4,16,2048]{2,1,0:T(8,128)S(1)} %get-tuple-element.64), channel_id=1, source_target_pairs={{8,16},{9,17},{10,18},{11,19},{12,20},{13,21},{14,22},{15,23},{0,2... | collective-permute-start | bytes 1572872 | tf_op jit(solution)/shard_map/ppermute | solution.py:626
  11.8 11.9 %collective-permute-start = (f32[4,8,2048]{2,1,0:T(8,128)S(1)}, f32[4,8,2048]{2,1,0:T(8,128)S(1)}, u32[]{:S(2)}, u32[]{:S(2)}) collective-permute-start(f32[4,8,2048]{2,1,0:T(8,128)S(1)} %get-tuple-element.57.sye), channel_id=1, source_target_pairs={{0,1},{2,3},{4,5},{6,7},{1,0},{3,2},{5,4},{7,6},{8,9},{10,11},{12,... | collective-permute-start | bytes 786440 | tf_op jit(solution)/shard_map/ppermute | solution.py:623
  12.9 17.2 %collective-permute-start.1 = (f32[4,8,2048]{2,1,0:T(8,128)S(1)}, f32[4,8,2048]{2,1,0:T(8,128)S(1)}, u32[]{:S(2)}, u32[]{:S(2)}) collective-permute-start(f32[4,8,2048]{2,1,0:T(8,128)S(1)} %get-tuple-element.58.syo), channel_id=1, source_target_pairs={{1,2},{9,10},{17,18},{25,26},{3,4},{11,12},{19,20},{27,28},{5,6},{... | collective-permute-start | bytes 786440 | tf_op jit(solution)/shard_map/ppermute | solution.py:624
  30.9 18.8 %collective-permute-start.6 = (f32[3,16,2048]{2,1,0:T(8,128)S(1)}, f32[3,16,2048]{2,1,0:T(8,128)S(1)}, u32[]{:S(2)}, u32[]{:S(2)}) collective-permute-start(f32[3,16,2048]{2,1,0:T(8,128)S(1)} %get-tuple-element.78), channel_id=1, source_target_pairs={{0,8},{16,24},{8,0},{24,16},{1,9},{17,25},{9,1},{25,17},{2,10},{18... | collective-permute-start | bytes 1179656 | tf_op jit(solution)/shard_map/ppermute | solution.py:625
  38.4 11.3 %collective-permute-start.7 = (f32[3,16,2048]{2,1,0:T(8,128)S(1)}, f32[3,16,2048]{2,1,0:T(8,128)S(1)}, u32[]{:S(2)}, u32[]{:S(2)}) collective-permute-start(f32[3,16,2048]{2,1,0:T(8,128)S(1)} %get-tuple-element.79), channel_id=1, source_target_pairs={{8,16},{9,17},{10,18},{11,19},{12,20},{13,21},{14,22},{15,23},{0,2... | collective-permute-start | bytes 1179656 | tf_op jit(solution)/shard_map/ppermute | solution.py:626
  39.3 10.4 %collective-permute-start.4 = (f32[3,8,2048]{2,1,0:T(8,128)S(1)}, f32[3,8,2048]{2,1,0:T(8,128)S(1)}, u32[]{:S(2)}, u32[]{:S(2)}) collective-permute-start(f32[3,8,2048]{2,1,0:T(8,128)S(1)} %get-tuple-element.65.sye), channel_id=1, source_target_pairs={{0,1},{2,3},{4,5},{6,7},{1,0},{3,2},{5,4},{7,6},{8,9},{10,11},{12,... | collective-permute-start | bytes 589832 | tf_op jit(solution)/shard_map/ppermute | solution.py:623
  40.8 8.9 %collective-permute-start.5 = (f32[3,8,2048]{2,1,0:T(8,128)S(1)}, f32[3,8,2048]{2,1,0:T(8,128)S(1)}, u32[]{:S(2)}, u32[]{:S(2)}) collective-permute-start(f32[3,8,2048]{2,1,0:T(8,128)S(1)} %get-tuple-element.66.syo), channel_id=1, source_target_pairs={{1,2},{9,10},{17,18},{25,26},{3,4},{11,12},{19,20},{27,28},{5,6},{... | collective-permute-start | bytes 589832 | tf_op jit(solution)/shard_map/ppermute | solution.py:624
  49.7 9.1 %copy-start.1 = (s32[8,16,2048]{2,1,0:T(8,128)S(1)}, s32[8,16,2048]{2,1,0:T(8,128)}, u32[]{:S(2)}) copy-start(s32[8,16,2048]{2,1,0:T(8,128)} %material.3) | copy-start | bytes 3145732
  49.7 9.1 %copy-start.2 = (f32[8,16,2048]{2,1,0:T(8,128)S(1)}, f32[8,16,2048]{2,1,0:T(8,128)}, u32[]{:S(2)}) copy-start(f32[8,16,2048]{2,1,0:T(8,128)} %history_old.1) | copy-start | bytes 3145732
  50.3 10.6 %collective-permute-start.8 = (f32[3,8,2048]{2,1,0:T(8,128)S(1)}, f32[3,8,2048]{2,1,0:T(8,128)S(1)}, u32[]{:S(2)}, u32[]{:S(2)}) collective-permute-start(f32[3,8,2048]{2,1,0:T(8,128)S(1)} %get-tuple-element.82.y_low), channel_id=1, source_target_pairs={{1,0},{2,1},{3,2},{4,3},{5,4},{6,5},{7,6},{9,8},{10,9},{11,10},{12... | collective-permute-start | bytes 589832 | tf_op jit(solution)/shard_map/ppermute | solution.py:632
  52.3 9.0 %collective-permute-start.9 = (f32[3,8,2048]{2,1,0:T(8,128)S(1)}, f32[3,8,2048]{2,1,0:T(8,128)S(1)}, u32[]{:S(2)}, u32[]{:S(2)}) collective-permute-start(f32[3,8,2048]{2,1,0:T(8,128)S(1)} %get-tuple-element.80.x_low0), channel_id=1, source_target_pairs={{8,0},{16,8},{24,16},{9,1},{17,9},{25,17},{10,2},{18,10},{26,18},{... | collective-permute-start | bytes 589832 | tf_op jit(solution)/shard_map/ppermute | solution.py:632
  56.9 7.0 %collective-permute-start.10 = (f32[3,8,2048]{2,1,0:T(8,128)S(1)}, f32[3,8,2048]{2,1,0:T(8,128)S(1)}, u32[]{:S(2)}, u32[]{:S(2)}) collective-permute-start(f32[3,8,2048]{2,1,0:T(8,128)S(1)} %get-tuple-element.81.x_low1), channel_id=1, source_target_pairs={{8,0},{16,8},{24,16},{9,1},{17,9},{25,17},{10,2},{18,10},{26,18},{... | collective-permute-start | bytes 589832 | tf_op jit(solution)/shard_map/ppermute | solution.py:632
  58.8 5.0 %copy-start.3 = (s32[1,12]{1,0:T(1,128)S(1)}, s32[1,12]{1,0:T(1,128)}, u32[]{:S(2)}) copy-start(s32[1,12]{1,0:T(1,128)} %ids.1) | copy-start | bytes 148
  58.8 5.0 %copy-start.4 = (s32[1,12,1]{1,2,0:T(1,128)S(1)}, s32[1,12,1]{1,2,0:T(1,128)}, u32[]{:S(2)}) copy-start(s32[1,12,1]{1,2,0:T(1,128)} %param.14) | copy-start | bytes 148
where the time goes:
time: 71.2 us; the launch traced here: 70.9 us
  starting transfers between devices  27.7 us (39%)
  waiting for transfers between devices  22.3 us (31%)
  Pallas kernels  20.1 us (28%)
  between operations  0.77 us (1%)
    pallas_call x7, Pallas kernels, call(): pl.pallas_call(kernel, out_shape=shapes, in_specs=in_specs, out_specs=out...  20.1 us
    ppermute x2, waiting for transfers between devices, exchange(): lax.ppermute(ye, 'yz', even_pairs('yz'))  12.8 us
    ppermute x2, starting transfers between devices, exchange(): lax.ppermute(xe, 'gx', even_pairs('gx'))  8.74 us
    ppermute x3, starting transfers between devices, from_above(): return lax.ppermute(value, axis, [(i + 1, i) for i in range(size - 1)])  8.48 us
    ppermute x2, waiting for transfers between devices, exchange(): lax.ppermute(yo, both, odd_pairs('yz'))  6.48 us
    all_to_all x1, starting transfers between devices, body(): lax.all_to_all(toughness[0], 'yz', split_axis=0, concat_axis=0, tiled=True)  5.73 us
    ppermute x3, waiting for transfers between devices, from_above(): return lax.ppermute(value, axis, [(i + 1, i) for i in range(size - 1)])  3 us
    ppermute x2, starting transfers between devices, exchange(): lax.ppermute(ye, 'yz', even_pairs('yz'))  2.67 us
  transfers between devices with their start and end apart: 12, of which 5 were waited for; matrix products, arithmetic and copies ran while one was open for 0% of the time, Pallas kernels for 18%

commit v1 on v0

--- a/solution.py
+++ b/solution.py
@@ -132,31 +132,37 @@
     def planes(low, high):
         for side, out in ((0, low), (nx - 1, high)):
             for t in range(nt):
-                for c in range(out.shape[0]):
-                    out[c, t * ROWS : (t + 1) * ROWS, :] = read(c, side, t)
+                for c in range(out[t].shape[0]):
+                    value = read(c, side, t)
+                    out[t][c, :, : value.shape[1]] = value
 
     by_parity(lax.axis_index("gx") % 2, even, odd, planes)
 
 
-def begin_kernel(damage, material, field, u, stiff, ye, yo, xe, xo, damage_kept, material_kept, sems):
+def far_copies(tough, d, far, sems, base):
+    me = lax.axis_index("yz")
+    return [pltpu.make_async_copy(tough.at[me ^ d ^ p], far.at[p], sems.at[base, p]) for p in (0, 1)]
+
+
+def begin_kernel(damage, material, field, tough, u, stiff, ye, yo, xe0, xe1, xo0, xo1, far_one, damage_kept, material_kept, sems):
     nx, ny, nz = stiff.shape
     nt = ny // ROWS
     copies = [
-        pltpu.make_async_copy(damage, damage_kept, sems.at[0]),
-        pltpu.make_async_copy(material, material_kept, sems.at[1]),
-        pltpu.make_async_copy(field, u, sems.at[2]),
+        [pltpu.make_async_copy(source.at[x], target.at[x], sems.at[i, x]) for x in range(nx)]
+        for i, (source, target) in enumerate(((damage, damage_kept), (material, material_kept)))
     ]
-    start_all(copies)
-    copies[0].wait()
-    copies[1].wait()
-
-    def plane(x, _):
+    fields = [pltpu.make_async_copy(field.at[c], u.at[c], sems.at[2, c]) for c in range(3)]
+    owed = far_copies(tough, routes(lax.axis_size("yz"))[0], far_one, sems, 3)
+    for pair in zip(*copies):
+        start_all(pair)
+    start_all(fields + owed)
+    for x in range(nx):
+        copies[0][x].wait()
+        copies[1][x].wait()
         d = 1.0 - damage_kept[x]
         stiff[x] = modulus(material_kept[x]) * (d * d + 0.001)
-        return 0
-
-    lax.fori_loop(0, nx, plane, 0)
-    copies[2].wait()
+    for copy in fields:
+        copy.wait()
 
     def rows(low, high):
         for side, out in ((0, low), (ny - 1, high)):
@@ -171,7 +177,9 @@
         part = slice(t * ROWS, (t + 1) * ROWS)
         return u[c, x, part, :] if c < 3 else stiff[x, part, :]
 
-    pack_planes(xe, xo, read, nx, nt)
+    pack_planes((xe0, xe1), (xo0, xo1), read, nx, nt)
+    for copy in owed:
+        copy.wait()
 
 
 def relax_inner(x, place, u, load, weights, scale, out, acc_x, acc_y, faces):
@@ -211,10 +219,14 @@
 
 
 def inner_one_kernel(
-    u, stiff, force, wx, wya, wyb, wza, wzb, scale, out, acc_x, acc_y, diag_x, diag_y, faces, diag_faces
+    u, stiff, force, tough, early0, early1, wx, wya, wyb, wza, wzb, scale, out, acc_x, acc_y, diag_x, diag_y, hop, faces, diag_faces, sems
 ):
     nx, ny, nz = stiff.shape
     nt, nk = ny // ROWS, nz // LANES
+    me = lax.axis_index("yz")
+    ways = routes(lax.axis_size("yz"))[1]
+    copies = [pltpu.make_async_copy(tough.at[me ^ 1 ^ d], hop.at[i], sems.at[i]) for i, d in enumerate(ways)]
+    start_all(copies)
 
     def prepare(x, place):
         lane, row = lane_index(), row_index()
@@ -269,6 +281,8 @@
     planes_of(nx, prepare)
     inner_pass(u, force, wx, wya, wyb, wza, wzb, scale, out, acc_x, acc_y, faces)
     compact_rows(diag_faces, diag_y, nx)
+    for copy in copies:
+        copy.wait()
 
 
 def inner_pass(u, force, wx, wya, wyb, wza, wzb, scale, out, acc_x, acc_y, faces):
@@ -299,13 +313,13 @@
 
 
 def face_one_kernel(
-    u, stiff, sye, syo, acc_x, acc_y, diag_x, diag_y, hye, hyo, hxe, hxo,
-    ye, yo, xe, xo, w_x, w_xy, s_x, w_y, w_yx, s_y, planes,
+    u, stiff, sye, syo, acc_x, acc_y, diag_x, diag_y, hxe0, hye, hyo, hxe1, hxo0, hxo1,
+    ye, yo, xe0, xe1, xo0, xo1, w_x, w_xy, s_x, w_y, w_yx, s_y, planes,
 ):
     _, nx, ny, nz = u.shape
     nt, nk = ny // ROWS, nz // LANES
     hy = Halo("yz", hye, hyo)
-    hx = Halo("gx", hxe, hxo)
+    hx = Halo("gx", (hxe0, hxe1), (hxo0, hxo1))
     row = row_index()
 
     def x_halo(side, c, t, k):
@@ -365,7 +379,7 @@
     def read(c, x, t):
         return planes[LOW if x == 0 else HIGH, c, t * ROWS : (t + 1) * ROWS, :]
 
-    pack_planes(xe, xo, read, nx, nt)
+    pack_planes((xe0, xe1), (xo0, xo1), read, nx, nt)
 
 
 def insert_faces(u, x_face, y_face):
@@ -390,22 +404,35 @@
 
 
 def inner_two_kernel(
-    u_in, scale, force, wx, wya, wyb, wza, wzb, sye, syo, planes,
-    u, out, acc_x, acc_y, faces,
+    u_in, scale, force, wx, wya, wyb, wza, wzb, sye, syo, planes, tough, hop, far_one, early0, early1,
+    u, out, acc_x, acc_y, hop_two, *rest,
 ):
+    *fars, faces, sems = rest
+    me = lax.axis_index("yz")
+    copies = [
+        pltpu.make_async_copy(tough.at[me ^ 1], hop_two.at[0], sems.at[2 * len(fars)]),
+        pltpu.make_async_copy(far_one.at[1], hop_two.at[1], sems.at[2 * len(fars) + 1]),
+    ]
+    for i, (d, far) in enumerate(zip(routes(lax.axis_size("yz"))[1], fars)):
+        copies.append(pltpu.make_async_copy(tough.at[me ^ d], far.at[0], sems.at[2 * i]))
+        copies.append(pltpu.make_async_copy(hop.at[i], far.at[1], sems.at[2 * i + 1]))
+    start_all(copies)
     hy = lax.axis_index("yz") % 2
     insert_faces(u, lambda side, c, t, k: tile(planes, (side, c), t, k), lambda side, c, k: own_side(hy, side, sye, syo, (c,), k))
     inner_pass(u, force, wx, wya, wyb, wza, wzb, scale, out, acc_x, acc_y, faces)
+    for copy in copies:
+        copy.wait()
 
 
 def face_two_kernel(
-    u, sye, syo, acc_x, acc_y, w_x, w_xy, s_x, w_y, w_yx, s_y, hye, hyo, hxe, hxo,
-    x_low0, x_low1, y_low, x_high, y_high,
+    u, sye, syo, acc_x, acc_y, w_x, w_xy, s_x, w_y, w_yx, s_y, hxe0, hye, hyo, hxe1, hxo0, hxo1, *rest
 ):
+    passed = (len(rest) - 5) // 2
+    x_low0, x_low1, y_low, x_high, y_high = rest[passed : passed + 5]
     _, nx, ny, nz = u.shape
     nt, nk = ny // ROWS, nz // LANES
     hy = Halo("yz", hye, hyo)
-    hx = Halo("gx", hxe, hxo)
+    hx = Halo("gx", (hxe0, hxe1), (hxo0, hxo1))
     row = row_index()
 
     def x_halo(side, c, t, k):
@@ -444,9 +471,9 @@
 
 
 def energy_kernel(
-    u_in, x_low0, x_low1, y_low, x_high, y_high, material, history_old,
-    u, u_out, history, top, half_top, far, half_far, rows, half_rows, sems,
+    u_in, x_low0, x_low1, y_low, x_high, y_high, material, history_old, tough_from, far_one, *rest
 ):
+    *fars, u, u_out, history, top, half_top, far, half_far, tough, rows, half_rows, sems = rest
     _, nx, ny, nz = u.shape
     nt, nk = ny // ROWS, nz // LANES
     x_low = (x_low0, x_low1)
@@ -455,7 +482,13 @@
         lambda side, c, t, k: x_part((x_low, x_high)[side], c, t, k),
         lambda side, c, k: tile((y_low, y_high)[side], (c,), 0, k),
     )
+    me, size = lax.axis_index("yz"), lax.axis_size("yz")
+    first, others = routes(size)
+    sources = {0: tough_from.at[me], first: far_one.at[0]}
+    for d, arrived in zip(others, fars):
+        sources.update({d: arrived.at[0], d ^ 1: arrived.at[1]})
     copies = [pltpu.make_async_copy(u.at[c], u_out.at[c], sems.at[c]) for c in range(3)]
+    copies += [pltpu.make_async_copy(source, tough.at[d], sems.at[3 + d]) for d, source in sources.items()]
     start_all(copies)
 
     def body(x, place):
@@ -498,20 +531,14 @@
         copy.wait()
 
 
-def last_kernel(
-    ids, owners, history_in, top, half_top, far, half_far, x_high, y_high, hy, hx0, hx1, tough_from, damage_from,
-    history, history_out, damage_out, energy, damage, tough, sems,
+def history_kernel(
+    history_in, top, half_top, far, half_far, x_high, y_high, hy, hx0, hx1, damage_from, history, damage, energy, sems
 ):
     nx, ny, nz = damage.shape
     nt, nk = ny // ROWS, nz // LANES
-    count = ids.shape[1]
     hx = (hx0, hx1)
-    fetched = [pltpu.make_async_copy(damage_from, damage, sems.at[2])]
-    for n in range(count):
-        owner = owners[0, n]
-        slot = sum([(owners[0, m] == owner).astype(jnp.int32) for m in range(n)], jnp.int32(0))
-        fetched.append(pltpu.make_async_copy(tough_from.at[owner, slot], tough.at[n], sems.at[3 + n]))
-    start_all(fetched)
+    copy = pltpu.make_async_copy(damage_from, damage, sems.at[0])
+    copy.start()
 
     def squares(here, beyond):
         return sum([(beyond(c) - here(c)) ** 2 for c in range(3)])
@@ -534,6 +561,16 @@
             if t == nt - 1:
                 total = total + jnp.where(row_index() == ROWS - 1, moved(y_term, nx - 1, ROWS - 1), 0.0)
             put(history, (nx - 1,), t, k, jnp.maximum(tile(history, (nx - 1,), t, k), tile(half_far, (), t, k) * total))
+    copy.wait()
+
+
+def last_kernel(ids, owners, history, damage_in, tough_in, hop_two, damage, tough, history_out, damage_out, sems):
+    nx, ny, nz = damage.shape
+    nt = ny // ROWS
+    count = ids.shape[1]
+    me, size = lax.axis_index("yz"), lax.axis_size("yz")
+    fetched = [pltpu.make_async_copy(hop_two.at[i], tough.at[d ^ 1], sems.at[2 + i]) for i, d in enumerate((0, routes(size)[0]))]
+    start_all(fetched)
     saved = pltpu.make_async_copy(history, history_out, sems.at[0])
     saved.start()
     for copy in fetched:
@@ -569,12 +606,14 @@
         states = []
         for p in range(per):
             n = q * per + p
+            owner = owners[0, n]
+            slot = lax.fori_loop(0, n, lambda m, found: found + (owners[0, m] == owner).astype(jnp.int32), jnp.int32(0))
             lanes = pl.ds(pl.multiple_of(ids[0, n] * LANES, LANES), LANES)
             first, second, d = {}, {}, {}
             for x, t in cells:
                 part = slice(t * ROWS, (t + 1) * ROWS)
                 h2 = 2.0 * history[x, part, lanes]
-                g = tough[n, x, part, :]
+                g = tough[owner ^ me, slot, x, part, :]
                 g2 = g * LENGTH
                 inverse = 1.0 / (g / LENGTH + h2 + 6.0 * g2)
                 first[x, t] = h2 * inverse
@@ -617,14 +656,25 @@
     return pairs + [(b, a) for a, b in pairs]
 
 
-def exchange(ye, yo, xe, xo):
+def exchange(ye, yo, xe0, xe1, xo0, xo1):
     both = ("gx", "yz")
     return (
+        lax.ppermute(xe0, "gx", even_pairs("gx")),
         lax.ppermute(ye, "yz", even_pairs("yz")),
         lax.ppermute(yo, both, odd_pairs("yz")),
-        lax.ppermute(xe, "gx", even_pairs("gx")),
-        lax.ppermute(xo, both, odd_pairs("gx")),
-    )
+        lax.ppermute(xe1, "gx", even_pairs("gx")),
+        lax.ppermute(xo0, both, odd_pairs("gx")),
+        lax.ppermute(xo1, both, odd_pairs("gx")),
+    )
+
+
+def routes(size):
+    assert size >= 8 and size & (size - 1) == 0
+    return 4, tuple(d for d in (6, 2) + tuple(range(8, size, 2)))
+
+
+def across(value, d):
+    return lax.ppermute(value, "yz", [(i, i ^ d) for i in range(lax.axis_size("yz"))])
 
 
 def from_above(value, axis):
@@ -669,60 +719,75 @@
     full, cells, halves = (3, nx, ny, nz), (nx, ny, nz), (3, ROWS, nz)
 
     def faces(count):
-        return here(*[(count, nx, nz)] * 2, *[(count, ny, nz)] * 2)
+        return here(*[(count, nx, nz)] * 2, *[(count, ROWS, nz)] * 2, *[(count, ROWS, nz + LANES)] * 2)
 
     def copies(count):
         return pltpu.SemaphoreType.DMA((count,))
 
-    arrived = lax.all_to_all(toughness[0], "yz", split_axis=0, concat_axis=0, tiled=True)
-    u, stiff, *sent = call(
+    tough = toughness[0]
+    pair = (2,) + tough.shape[1:]
+    first, others = routes(lax.axis_size("yz"))
+    u, stiff, *sent, far_one = call(
         begin_kernel,
-        here(full, cells) + faces(4),
-        far_off(damage, material, displacement),
-        [pltpu.VMEM(cells, F32), pltpu.VMEM(cells, jnp.int32), copies(3)],
+        here(full, cells) + faces(4) + here(pair),
+        far_off(damage, material, displacement, tough),
+        [pltpu.VMEM(cells, F32), pltpu.VMEM(cells, jnp.int32), pltpu.SemaphoreType.DMA((4, nx))],
     )
     brought = exchange(*sent)
-    wx, wya, wyb, wza, wzb, scale, u1, acc_x, acc_y, diag_x, diag_y = call(
+    far_one = across(far_one, first)
+    wx, wya, wyb, wza, wzb, scale, u1, acc_x, acc_y, diag_x, diag_y, hop = call(
         inner_one_kernel,
-        here((nx - 1, ny, nz), *[cells] * 5, full, (2, 3, ny, nz), (2, 3, nx, nz), (2, ny, nz), (2, 1, nx, nz)),
-        kept(u, stiff, force),
-        [pltpu.VMEM((2, 3, nx, ROWS, nz), F32), pltpu.VMEM((2, 1, nx, ROWS, nz), F32)],
-    )
+        here((nx - 1, ny, nz), *[cells] * 5, full, (2, 3, ny, nz), (2, 3, nx, nz), (2, ny, nz), (2, 1, nx, nz))
+        + here((len(others),) + tough.shape[1:]),
+        kept(u, stiff, force) + far_off(tough) + kept(brought[0], brought[3]),
+        [pltpu.VMEM((2, 3, nx, ROWS, nz), F32), pltpu.VMEM((2, 1, nx, ROWS, nz), F32), copies(len(others))],
+    )
+    hop = across(hop, 1)
     *own, w_x, w_xy, s_x, w_y, w_yx, s_y, planes = call(
         face_one_kernel,
         faces(3) + here(*[(2, ny, nz)] * 3, *[(2, nx, nz)] * 3, (2, 3, ny, nz)),
         kept(u, stiff, sent[0], sent[1], acc_x, acc_y, diag_x, diag_y, *brought),
     )
     brought = exchange(*own)
-    u1, u2, acc_x, acc_y = call(
+    u1, u2, acc_x, acc_y, hop_two, *fars = call(
         inner_two_kernel,
-        here(full, full, (2, 3, ny, nz), (2, 3, nx, nz)),
-        kept(u1, scale, force, wx, wya, wyb, wza, wzb, own[0], own[1], planes),
-        [pltpu.VMEM((2, 3, nx, ROWS, nz), F32)],
+        here(full, full, (2, 3, ny, nz), (2, 3, nx, nz), pair, *[pair for _ in others]),
+        kept(u1, scale, force, wx, wya, wyb, wza, wzb, own[0], own[1], planes)
+        + far_off(tough)
+        + kept(hop, far_one, brought[0], brought[3]),
+        [pltpu.VMEM((2, 3, nx, ROWS, nz), F32), copies(2 + 2 * len(others))],
         {0: 0},
     )
-    x_low0, x_low1, y_low, x_high, y_high = call(
+    lasts = [across(value, d) for d, value in zip(others, fars)]
+    x_low0, x_low1, y_low, x_high, y_high, hop_two = call(
         face_two_kernel,
-        here(halves, halves, (3, nx, nz), (3, ny, nz), (3, nx, nz)),
-        kept(u1, own[0], own[1], acc_x, acc_y, w_x, w_xy, s_x, w_y, w_yx, s_y, *brought),
-    )
+        here(halves, halves, (3, nx, nz), (3, ny, nz), (3, nx, nz), hop_two.shape),
+        kept(u1, own[0], own[1], acc_x, acc_y, w_x, w_xy, s_x, w_y, w_yx, s_y, *brought, hop_two),
+        (),
+        {17: 5},
+    )
+    hop_two = across(hop_two, 1)
     hy, hx0, hx1 = from_above(y_low, "yz"), from_above(x_low0, "gx"), from_above(x_low1, "gx")
-    _, new_displacement, history, *sums = call(
+    _, new_displacement, history, *sums, tough_kept = call(
         energy_kernel,
-        here(full) + [(full, HBM)] + here(cells, *[(nx, nz)] * 2, *[(ny, nz)] * 2),
-        kept(u2, x_low0, x_low1, y_low, x_high, y_high, material, history_old),
-        [pltpu.VMEM((nx, ROWS, nz), F32), pltpu.VMEM((nx, ROWS, nz), F32), copies(3)],
+        here(full) + [(full, HBM)] + here(cells, *[(nx, nz)] * 2, *[(ny, nz)] * 2, tough.shape),
+        kept(u2, x_low0, x_low1, y_low, x_high, y_high, material, history_old) + far_off(tough) + kept(far_one, *lasts),
+        [pltpu.VMEM((nx, ROWS, nz), F32), pltpu.VMEM((nx, ROWS, nz), F32), copies(3 + tough.shape[0])],
         {0: 0},
     )
-    count = patch_ids.shape[1]
-    _, new_history, new_damage = call(
+    history, damage_kept = call(
+        history_kernel,
+        here(cells, cells),
+        kept(history, *sums, x_high, y_high, hy, hx0, hx1) + far_off(damage),
+        [pltpu.VMEM((nx, nz), F32), copies(1)],
+        {0: 0},
+    )
+    _, _, new_history, new_damage = call(
         last_kernel,
-        here(cells) + [(cells, HBM), (cells, HBM)],
-        [(patch_ids, pltpu.SMEM), (owners[:, :, 0], pltpu.SMEM)]
-        + kept(history, *sums, x_high, y_high, hy, hx0, hx1)
-        + far_off(arrived, damage),
-        [pltpu.VMEM((nx, nz), F32), pltpu.VMEM(cells, F32), pltpu.VMEM((count,) + arrived.shape[2:], F32), copies(3 + count)],
-        {2: 0},
+        here(cells, tough.shape) + [(cells, HBM), (cells, HBM)],
+        [(patch_ids, pltpu.SMEM), (owners[:, :, 0], pltpu.SMEM)] + kept(history, damage_kept, tough_kept, hop_two),
+        [copies(4)],
+        {3: 0, 4: 1},
     )
     return (new_displacement, new_history, new_damage)
 

time: 71.2 us -> 63.9 us (0.90)
  the two profiles are of different devices: /device:TPU:9 before, /device:TPU:0 now
where the time goes in v1:
time: 63.9 us; the launch traced here: 63.7 us
  starting transfers between devices  30.1 us (47%)
  Pallas kernels  22.4 us (35%)
  waiting for transfers between devices  10.4 us (16%)
  between operations  0.84 us (1%)
    pallas_call x8, Pallas kernels, call(): pl.pallas_call(kernel, out_shape=shapes, in_specs=in_specs, out_specs=out...  22.4 us
    ppermute x5, starting transfers between devices, across(): lax.ppermute(value, 'yz', [(i, i ^ d) for i in range(lax.axis_size('yz'))])  10.5 us
    ppermute x2, starting transfers between devices, exchange(): lax.ppermute(xo0, both, odd_pairs('gx'))  7.17 us
    ppermute x2, starting transfers between devices, exchange(): lax.ppermute(ye, 'yz', even_pairs('yz'))  5.15 us
    ppermute x5, waiting for transfers between devices, across(): lax.ppermute(value, 'yz', [(i, i ^ d) for i in range(lax.axis_size('yz'))])  4.92 us
    ppermute x3, starting transfers between devices, from_above(): return lax.ppermute(value, axis, [(i + 1, i) for i in range(size - 1)])  3.85 us
    ppermute x2, waiting for transfers between devices, exchange(): lax.ppermute(xo1, both, odd_pairs('gx'))  3.06 us
    ppermute x2, waiting for transfers between devices, exchange(): lax.ppermute(ye, 'yz', even_pairs('yz'))  2.37 us
  transfers between devices with their start and end apart: 20, of which 4 were waited for; matrix products, arithmetic and copies ran while one was open for 0% of the time, Pallas kernels for 21%

profile of v1, /device:TPU:0, one launch (start us, length us, event | category | flops | bytes accessed | tf_op | source)
XLA Modules:
  0.0 63.7 jit_solution(10879699533446772589)
XLA Ops:
  0.6 3.2 %shard_map.103 = (f32[3,8,16,2048]{3,2,1,0:T(8,128)S(1)}, f32[8,16,2048]{2,1,0:T(8,128)S(1)}, f32[4,8,2048]{2,1,0:T(8,128)S(1)}, f32[4,8,2048]{2,1,0:T(8,128)S(1...) custom-call(f32[8,16,2048]{2,1,0:T(8,128)} %damage_from.1, ...), custom_call_target="tpu_custom_call" | custom-call | tf_op jit(solution)/shard_map/pallas_call | solution.py:693
  3.9 0.5 collective-permute-start
  4.4 0.1 collective-permute-start.1
  4.5 2.9 %collective-permute-start.2 = (f32[4,8,2048]{2,1,0:T(8,128)S(1)}, f32[4,8,2048]{2,1,0:T(8,128)S(1)}, u32[]{:S(2)}, u32[]{:S(2)}) collective-permute-start(f32[4,8,2048]{2,1,0:T(8,128)S(1)} %get-tuple-element.72.sye), channel_id=1, source_target_pairs={{0,1},{2,3},{4,5},{6,7},{1,0},{3,2},{5,4},{7,6},{8,9},{10,11},{12,... | collective-permute-start | bytes 786440 | tf_op jit(solution)/shard_map/ppermute | solution.py:663
  7.4 1.6 %collective-permute-start.4 = (f32[4,8,2176]{2,1,0:T(8,128)S(1)}, f32[4,8,2176]{2,1,0:T(8,128)S(1)}, u32[]{:S(2)}, u32[]{:S(2)}) collective-permute-start(f32[4,8,2176]{2,1,0:T(8,128)S(1)} %get-tuple-element.78), channel_id=1, source_target_pairs={{8,16},{9,17},{10,18},{11,19},{12,20},{13,21},{14,22},{15,23},{0,2... | collective-permute-start | bytes 835592 | tf_op jit(solution)/shard_map/ppermute | solution.py:666
  9.0 0.4 collective-permute-start.5
  9.5 3.0 %collective-permute-start.7 = (f32[2,2,8,16,128]{4,3,2,1,0:T(8,128)S(1)}, f32[2,2,8,16,128]{4,3,2,1,0:T(8,128)S(1)}, u32[]{:S(2)}, u32[]{:S(2)}) collective-permute-start(f32[2,2,8,16,128]{4,3,2,1,0:T(8,128)S(1)} %get-tuple-element.84), channel_id=1, source_target_pairs={{0,4},{1,5},{2,6},{3,7},{4,0},{5,1},{6,2},{7,3},{8,12},{9,13},{10,... | collective-permute-start | bytes 786440 | tf_op jit(solution)/shard_map/ppermute | solution.py:677
  12.5 3.9 %shard_map.104 = (f32[7,16,2048]{2,1,0:T(8,128)S(1)}, f32[8,16,2048]{2,1,0:T(8,128)S(1)}, f32[8,16,2048]{2,1,0:T(8,128)S(1)}, f32[8,16,2048]{2,1,0:T(8,128)S(1)}...) custom-call(f32[3,8,16,2048]{3,2,1,0:T(8,128)S(1)} %get-tuple-elemen, ...), custom_call_target="tpu_custom_call" | custom-call | tf_op jit(solution)/shard_map/pallas_call | solution.py:693
  16.4 2.7 %collective-permute-start.6 = (f32[2,2,8,16,128]{4,3,2,1,0:T(8,128)S(1)}, f32[2,2,8,16,128]{4,3,2,1,0:T(8,128)S(1)}, u32[]{:S(2)}, u32[]{:S(2)}) collective-permute-start(f32[2,2,8,16,128]{4,3,2,1,0:T(8,128)S(1)} %get-tuple-element.83), channel_id=1, source_target_pairs={{0,1},{1,0},{2,3},{3,2},{4,5},{5,4},{6,7},{7,6},{8,9},{9,8},{10,11... | collective-permute-start | bytes 786440 | tf_op jit(solution)/shard_map/ppermute | solution.py:677
  19.1 3.1 %collective-permute-done.5.hxo1 = f32[4,8,2176]{2,1,0:T(8,128)S(1)} collective-permute-done((f32[4,8,2176]{2,1,0:T(8,128)S(1)}, f32[4,8,2176]{2,1,0:T(8,128)S(1)}, u32[]{:S(2)}, u32[]{:S(2)}) %collective-permute-start.5) | collective-permute-done | bytes 278560 | tf_op jit(solution)/shard_map/ppermute | solution.py:667
  22.2 0.7 %shard_map.105 = (f32[3,8,2048]{2,1,0:T(8,128)S(1)}, f32[3,8,2048]{2,1,0:T(8,128)S(1)}, f32[3,8,2048]{2,1,0:T(8,128)S(1)}, f32[3,8,2048]{2,1,0:T(8,128)S(1)}, f3...) custom-call(f32[3,8,16,2048]{3,2,1,0:T(8,128)S(1)} %get-tuple-elemen, ...), custom_call_target="tpu_custom_call" | custom-call | tf_op jit(solution)/shard_map/pallas_call | solution.py:693
  22.9 0.1 collective-permute-start.8
  23.0 0.5 collective-permute-start.9
  23.5 5.6 %collective-permute-start.12 = (f32[3,8,2176]{2,1,0:T(8,128)S(1)}, f32[3,8,2176]{2,1,0:T(8,128)S(1)}, u32[]{:S(2)}, u32[]{:S(2)}) collective-permute-start(f32[3,8,2176]{2,1,0:T(8,128)S(1)} %get-tuple-element.97), channel_id=1, source_target_pairs={{8,16},{9,17},{10,18},{11,19},{12,20},{13,21},{14,22},{15,23},{0,2... | collective-permute-start | bytes 626696 | tf_op jit(solution)/shard_map/ppermute | solution.py:666
  29.1 1.7 %collective-permute-start.13 = (f32[3,8,2176]{2,1,0:T(8,128)S(1)}, f32[3,8,2176]{2,1,0:T(8,128)S(1)}, u32[]{:S(2)}, u32[]{:S(2)}) collective-permute-start(f32[3,8,2176]{2,1,0:T(8,128)S(1)} %get-tuple-element.98), channel_id=1, source_target_pairs={{8,16},{9,17},{10,18},{11,19},{12,20},{13,21},{14,22},{15,23},{0,2... | collective-permute-start | bytes 626696 | tf_op jit(solution)/shard_map/ppermute | solution.py:667
  30.8 2.2 %collective-permute-start.10 = (f32[3,8,2048]{2,1,0:T(8,128)S(1)}, f32[3,8,2048]{2,1,0:T(8,128)S(1)}, u32[]{:S(2)}, u32[]{:S(2)}) collective-permute-start(f32[3,8,2048]{2,1,0:T(8,128)S(1)} %get-tuple-element.80.sye), channel_id=1, source_target_pairs={{0,1},{2,3},{4,5},{6,7},{1,0},{3,2},{5,4},{7,6},{8,9},{10,11},{12,... | collective-permute-start | bytes 589832 | tf_op jit(solution)/shard_map/ppermute | solution.py:663
  33.1 3.6 %shard_map.106 = (f32[3,8,16,2048]{3,2,1,0:T(8,128)S(1)}, f32[3,8,16,2048]{3,2,1,0:T(8,128)S(1)}, f32[2,3,16,2048]{3,2,1,0:T(8,128)S(1)}, f32[2,3,8,2048]{3,2,1,...) custom-call(f32[3,8,16,2048]{3,2,1,0:T(8,128)S(1)} %get-tuple-elemen, ...), custom_call_target="tpu_custom_call", output_to_operand_aliasing={{0}: (0, {})} | custom-call | tf_op jit(solution)/shard_map/pallas_call | solution.py:693
  36.7 2.3 %collective-permute-start.14 = (f32[2,2,8,16,128]{4,3,2,1,0:T(8,128)S(1)}, f32[2,2,8,16,128]{4,3,2,1,0:T(8,128)S(1)}, u32[]{:S(2)}, u32[]{:S(2)}) collective-permute-start(f32[2,2,8,16,128]{4,3,2,1,0:T(8,128)S(1)} %get-tuple-element.105), channel_id=1, source_target_pairs={{0,6},{1,7},{2,4},{3,5},{4,2},{5,3},{6,0},{7,1},{8,14},{9,15},{10,... | collective-permute-start | bytes 786440 | tf_op jit(solution)/shard_map/ppermute | solution.py:677
  39.0 2.4 %collective-permute-done.10.hye = f32[3,8,2048]{2,1,0:T(8,128)S(1)} collective-permute-done((f32[3,8,2048]{2,1,0:T(8,128)S(1)}, f32[3,8,2048]{2,1,0:T(8,128)S(1)}, u32[]{:S(2)}, u32[]{:S(2)}) %collective-permute-start.10) | collective-permute-done | bytes 196640 | tf_op jit(solution)/shard_map/ppermute | solution.py:663
  41.4 0.0 copy-start.1
  41.4 0.0 copy-start.2
  41.4 0.7 %shard_map.107 = (f32[3,8,2048]{2,1,0:T(8,128)S(1)}, f32[3,8,2048]{2,1,0:T(8,128)S(1)}, f32[3,8,2048]{2,1,0:T(8,128)S(1)}, f32[3,16,2048]{2,1,0:T(8,128)S(1)}, f...) custom-call(f32[3,8,16,2048]{3,2,1,0:T(8,128)S(1)} %get-tuple-element.88.u, ...), custom_call_target="tpu_custom_call", output_to_operand_aliasing={{5}: (17, {})} | custom-call | tf_op jit(solution)/shard_map/pallas_call | solution.py:693
  42.1 2.5 %collective-permute-start.19 = (f32[2,2,8,16,128]{4,3,2,1,0:T(8,128)S(1)}, f32[2,2,8,16,128]{4,3,2,1,0:T(8,128)S(1)}, u32[]{:S(2)}, u32[]{:S(2)}) collective-permute-start(f32[2,2,8,16,128]{4,3,2,1,0:T(8,128)S(1)} %get-tuple-element.116), channel_id=1, source_target_pairs={{0,1},{1,0},{2,3},{3,2},{4,5},{5,4},{6,7},{7,6},{8,9},{9,8},{10,11... | collective-permute-start | bytes 786440 | tf_op jit(solution)/shard_map/ppermute | solution.py:677
  44.6 1.3 %collective-permute-start.16 = (f32[3,8,2048]{2,1,0:T(8,128)S(1)}, f32[3,8,2048]{2,1,0:T(8,128)S(1)}, u32[]{:S(2)}, u32[]{:S(2)}) collective-permute-start(f32[3,8,2048]{2,1,0:T(8,128)S(1)} %get-tuple-element.102.y_low), channel_id=1, source_target_pairs={{1,0},{2,1},{3,2},{4,3},{5,4},{6,5},{7,6},{9,8},{10,9},{11,10},{12... | collective-permute-start | bytes 589832 | tf_op jit(solution)/shard_map/ppermute | solution.py:682
  45.9 1.3 %collective-permute-start.17 = (f32[3,8,2048]{2,1,0:T(8,128)S(1)}, f32[3,8,2048]{2,1,0:T(8,128)S(1)}, u32[]{:S(2)}, u32[]{:S(2)}) collective-permute-start(f32[3,8,2048]{2,1,0:T(8,128)S(1)} %get-tuple-element.100.x_low0), channel_id=1, source_target_pairs={{8,0},{16,8},{24,16},{9,1},{17,9},{25,17},{10,2},{18,10},{26,18},{... | collective-permute-start | bytes 589832 | tf_op jit(solution)/shard_map/ppermute | solution.py:682
  47.2 0.8 %collective-permute-done.14.rest_0_ = f32[2,2,8,16,128]{4,3,2,1,0:T(8,128)S(1)} collective-permute-done((f32[2,2,8,16,128]{4,3,2,1,0:T(8,128)S(1)}, f32[2,2,8,16,128]{4,3,2,1,0:T(8,128)S(1)}, u32[]{:S(2)}, u32[]{:S(2)}) %collective-permute-start.14) | collective-permute-done | bytes 262176 | tf_op jit(solution)/shard_map/ppermute | solution.py:677
  48.0 1.3 %collective-permute-start.18 = (f32[3,8,2048]{2,1,0:T(8,128)S(1)}, f32[3,8,2048]{2,1,0:T(8,128)S(1)}, u32[]{:S(2)}, u32[]{:S(2)}) collective-permute-start(f32[3,8,2048]{2,1,0:T(8,128)S(1)} %get-tuple-element.101.x_low1), channel_id=1, source_target_pairs={{8,0},{16,8},{24,16},{9,1},{17,9},{25,17},{10,2},{18,10},{26,18},{... | collective-permute-start | bytes 589832 | tf_op jit(solution)/shard_map/ppermute | solution.py:682
  49.3 4.1 %collective-permute-done.15.rest_1_ = f32[2,2,8,16,128]{4,3,2,1,0:T(8,128)S(1)} collective-permute-done((f32[2,2,8,16,128]{4,3,2,1,0:T(8,128)S(1)}, f32[2,2,8,16,128]{4,3,2,1,0:T(8,128)S(1)}, u32[]{:S(2)}, u32[]{:S(2)}) %collective-permute-start.15) | collective-permute-done | bytes 262176 | tf_op jit(solution)/shard_map/ppermute | solution.py:677
  53.4 2.9 %shard_map.108 = (f32[3,8,16,2048]{3,2,1,0:T(8,128)S(1)}, f32[3,8,16,2048]{3,2,1,0:T(8,128)}, f32[8,16,2048]{2,1,0:T(8,128)S(1)}, f32[8,2048]{1,0:T(8,128)S(1)},...) custom-call(f32[3,8,16,2048]{3,2,1,0:T(8,128)S(1)} %get-tuple-elemen, ...), custom_call_target="tpu_custom_call", output_to_operand_aliasing={{0}: (0, {})} | custom-call | tf_op jit(solution)/shard_map/pallas_call | solution.py:693
  56.4 0.0 copy-start.3
  56.4 1.2 %shard_map.109 = (f32[8,16,2048]{2,1,0:T(8,128)S(1)}, f32[8,16,2048]{2,1,0:T(8,128)S(1)}) custom-call(f32[8,16,2048]{2,1,0:T(8,128)S(1)} %get-tuple-element.108.history_in, f32[8,2048]{1,0:T(8,128)S(1)} %get-tuple-element.109.top, f32[8,2048]{1,0:T(8,128)S(1)} %get-tuple-element.110.half_top, ...), custom_call_target="tpu_custom_call", output_to_operand_aliasing={{0}: (0, {})} | custom-call | tf_op jit(solution)/shard_map/pallas_call | solution.py:693
  57.7 6.0 %shard_map.110 = (f32[8,16,2048]{2,1,0:T(8,128)S(1)}, f32[8,2,8,16,128]{4,3,2,1,0:T(8,128)S(1)}, f32[8,16,2048]{2,1,0:T(8,128)}, f32[8,16,2048]{2,1,0:T(8,128)}) custom-call(s32[1,12]{1,0:T(1,128)S(1)} %copy-done.3, s32[1,12]{1,0:T(1,128)S(1)} %bitcast.2, ...), custom_call_target="tpu_custom_call", output_to_operand_aliasing={{0}: (3, {}), {1}: (4, {})} | custom-call | tf_op jit(solution)/shard_map/pallas_call | solution.py:693
  (26 shorter events, 0.1 us)
Async XLA Ops:
  0.6 11.8 %copy-start = (f32[3,8,16,2048]{3,2,1,0:T(8,128)S(1)}, f32[3,8,16,2048]{3,2,1,0:T(8,128)}, u32[]{:S(2)}) copy-start(f32[3,8,16,2048]{3,2,1,0:T(8,128)} %force.3) | copy-start | bytes 9437188
  3.9 5.6 %collective-permute-start = (f32[4,8,2048]{2,1,0:T(8,128)S(1)}, f32[4,8,2048]{2,1,0:T(8,128)S(1)}, u32[]{:S(2)}, u32[]{:S(2)}) collective-permute-start(f32[4,8,2048]{2,1,0:T(8,128)S(1)} %get-tuple-element.63), channel_id=1, source_target_pairs={{0,8},{16,24},{8,0},{24,16},{1,9},{17,25},{9,1},{25,17},{2,10},{18... | collective-permute-start | bytes 786440 | tf_op jit(solution)/shard_map/ppermute | solution.py:662
  4.4 5.1 %collective-permute-start.1 = (f32[4,8,2048]{2,1,0:T(8,128)S(1)}, f32[4,8,2048]{2,1,0:T(8,128)S(1)}, u32[]{:S(2)}, u32[]{:S(2)}) collective-permute-start(f32[4,8,2048]{2,1,0:T(8,128)S(1)} %get-tuple-element.64), channel_id=1, source_target_pairs={{0,8},{16,24},{8,0},{24,16},{1,9},{17,25},{9,1},{25,17},{2,10},{18... | collective-permute-start | bytes 786440 | tf_op jit(solution)/shard_map/ppermute | solution.py:665
  4.5 11.9 %collective-permute-start.2 = (f32[4,8,2048]{2,1,0:T(8,128)S(1)}, f32[4,8,2048]{2,1,0:T(8,128)S(1)}, u32[]{:S(2)}, u32[]{:S(2)}) collective-permute-start(f32[4,8,2048]{2,1,0:T(8,128)S(1)} %get-tuple-element.72.sye), channel_id=1, source_target_pairs={{0,1},{2,3},{4,5},{6,7},{1,0},{3,2},{5,4},{7,6},{8,9},{10,11},{12,... | collective-permute-start | bytes 786440 | tf_op jit(solution)/shard_map/ppermute | solution.py:663
  7.4 11.7 %collective-permute-start.4 = (f32[4,8,2176]{2,1,0:T(8,128)S(1)}, f32[4,8,2176]{2,1,0:T(8,128)S(1)}, u32[]{:S(2)}, u32[]{:S(2)}) collective-permute-start(f32[4,8,2176]{2,1,0:T(8,128)S(1)} %get-tuple-element.78), channel_id=1, source_target_pairs={{8,16},{9,17},{10,18},{11,19},{12,20},{13,21},{14,22},{15,23},{0,2... | collective-permute-start | bytes 835592 | tf_op jit(solution)/shard_map/ppermute | solution.py:666
  9.0 13.2 %collective-permute-start.5 = (f32[4,8,2176]{2,1,0:T(8,128)S(1)}, f32[4,8,2176]{2,1,0:T(8,128)S(1)}, u32[]{:S(2)}, u32[]{:S(2)}) collective-permute-start(f32[4,8,2176]{2,1,0:T(8,128)S(1)} %get-tuple-element.79), channel_id=1, source_target_pairs={{8,16},{9,17},{10,18},{11,19},{12,20},{13,21},{14,22},{15,23},{0,2... | collective-permute-start | bytes 835592 | tf_op jit(solution)/shard_map/ppermute | solution.py:667
  9.5 9.6 %collective-permute-start.3 = (f32[4,8,2048]{2,1,0:T(8,128)S(1)}, f32[4,8,2048]{2,1,0:T(8,128)S(1)}, u32[]{:S(2)}, u32[]{:S(2)}) collective-permute-start(f32[4,8,2048]{2,1,0:T(8,128)S(1)} %get-tuple-element.73.syo), channel_id=1, source_target_pairs={{1,2},{9,10},{17,18},{25,26},{3,4},{11,12},{19,20},{27,28},{5,6},{... | collective-permute-start | bytes 786440 | tf_op jit(solution)/shard_map/ppermute | solution.py:664
  9.5 19.6 %collective-permute-start.7 = (f32[2,2,8,16,128]{4,3,2,1,0:T(8,128)S(1)}, f32[2,2,8,16,128]{4,3,2,1,0:T(8,128)S(1)}, u32[]{:S(2)}, u32[]{:S(2)}) collective-permute-start(f32[2,2,8,16,128]{4,3,2,1,0:T(8,128)S(1)} %get-tuple-element.84), channel_id=1, source_target_pairs={{0,4},{1,5},{2,6},{3,7},{4,0},{5,1},{6,2},{7,3},{8,12},{9,13},{10,... | collective-permute-start | bytes 786440 | tf_op jit(solution)/shard_map/ppermute | solution.py:677
  16.4 16.7 %collective-permute-start.6 = (f32[2,2,8,16,128]{4,3,2,1,0:T(8,128)S(1)}, f32[2,2,8,16,128]{4,3,2,1,0:T(8,128)S(1)}, u32[]{:S(2)}, u32[]{:S(2)}) collective-permute-start(f32[2,2,8,16,128]{4,3,2,1,0:T(8,128)S(1)} %get-tuple-element.83), channel_id=1, source_target_pairs={{0,1},{1,0},{2,3},{3,2},{4,5},{5,4},{6,7},{7,6},{8,9},{9,8},{10,11... | collective-permute-start | bytes 786440 | tf_op jit(solution)/shard_map/ppermute | solution.py:677
  22.9 7.9 %collective-permute-start.8 = (f32[3,8,2048]{2,1,0:T(8,128)S(1)}, f32[3,8,2048]{2,1,0:T(8,128)S(1)}, u32[]{:S(2)}, u32[]{:S(2)}) collective-permute-start(f32[3,8,2048]{2,1,0:T(8,128)S(1)} %get-tuple-element.85), channel_id=1, source_target_pairs={{0,8},{16,24},{8,0},{24,16},{1,9},{17,25},{9,1},{25,17},{2,10},{18... | collective-permute-start | bytes 589832 | tf_op jit(solution)/shard_map/ppermute | solution.py:662
  23.0 10.1 %collective-permute-start.9 = (f32[3,8,2048]{2,1,0:T(8,128)S(1)}, f32[3,8,2048]{2,1,0:T(8,128)S(1)}, u32[]{:S(2)}, u32[]{:S(2)}) collective-permute-start(f32[3,8,2048]{2,1,0:T(8,128)S(1)} %get-tuple-element.86), channel_id=1, source_target_pairs={{0,8},{16,24},{8,0},{24,16},{1,9},{17,25},{9,1},{25,17},{2,10},{18... | collective-permute-start | bytes 589832 | tf_op jit(solution)/shard_map/ppermute | solution.py:665
  23.5 17.9 %collective-permute-start.12 = (f32[3,8,2176]{2,1,0:T(8,128)S(1)}, f32[3,8,2176]{2,1,0:T(8,128)S(1)}, u32[]{:S(2)}, u32[]{:S(2)}) collective-permute-start(f32[3,8,2176]{2,1,0:T(8,128)S(1)} %get-tuple-element.97), channel_id=1, source_target_pairs={{8,16},{9,17},{10,18},{11,19},{12,20},{13,21},{14,22},{15,23},{0,2... | collective-permute-start | bytes 626696 | tf_op jit(solution)/shard_map/ppermute | solution.py:666
  29.1 12.3 %collective-permute-start.13 = (f32[3,8,2176]{2,1,0:T(8,128)S(1)}, f32[3,8,2176]{2,1,0:T(8,128)S(1)}, u32[]{:S(2)}, u32[]{:S(2)}) collective-permute-start(f32[3,8,2176]{2,1,0:T(8,128)S(1)} %get-tuple-element.98), channel_id=1, source_target_pairs={{8,16},{9,17},{10,18},{11,19},{12,20},{13,21},{14,22},{15,23},{0,2... | collective-permute-start | bytes 626696 | tf_op jit(solution)/shard_map/ppermute | solution.py:667
  30.8 10.6 %collective-permute-start.10 = (f32[3,8,2048]{2,1,0:T(8,128)S(1)}, f32[3,8,2048]{2,1,0:T(8,128)S(1)}, u32[]{:S(2)}, u32[]{:S(2)}) collective-permute-start(f32[3,8,2048]{2,1,0:T(8,128)S(1)} %get-tuple-element.80.sye), channel_id=1, source_target_pairs={{0,1},{2,3},{4,5},{6,7},{1,0},{3,2},{5,4},{7,6},{8,9},{10,11},{12,... | collective-permute-start | bytes 589832 | tf_op jit(solution)/shard_map/ppermute | solution.py:663
  33.1 8.3 %collective-permute-start.11 = (f32[3,8,2048]{2,1,0:T(8,128)S(1)}, f32[3,8,2048]{2,1,0:T(8,128)S(1)}, u32[]{:S(2)}, u32[]{:S(2)}) collective-permute-start(f32[3,8,2048]{2,1,0:T(8,128)S(1)} %get-tuple-element.81.syo), channel_id=1, source_target_pairs={{1,2},{9,10},{17,18},{25,26},{3,4},{11,12},{19,20},{27,28},{5,6},{... | collective-permute-start | bytes 589832 | tf_op jit(solution)/shard_map/ppermute | solution.py:664
  36.7 11.3 %collective-permute-start.14 = (f32[2,2,8,16,128]{4,3,2,1,0:T(8,128)S(1)}, f32[2,2,8,16,128]{4,3,2,1,0:T(8,128)S(1)}, u32[]{:S(2)}, u32[]{:S(2)}) collective-permute-start(f32[2,2,8,16,128]{4,3,2,1,0:T(8,128)S(1)} %get-tuple-element.105), channel_id=1, source_target_pairs={{0,6},{1,7},{2,4},{3,5},{4,2},{5,3},{6,0},{7,1},{8,14},{9,15},{10,... | collective-permute-start | bytes 786440 | tf_op jit(solution)/shard_map/ppermute | solution.py:677
  41.4 12.0 %collective-permute-start.15 = (f32[2,2,8,16,128]{4,3,2,1,0:T(8,128)S(1)}, f32[2,2,8,16,128]{4,3,2,1,0:T(8,128)S(1)}, u32[]{:S(2)}, u32[]{:S(2)}) collective-permute-start(f32[2,2,8,16,128]{4,3,2,1,0:T(8,128)S(1)} %get-tuple-element.106), channel_id=1, source_target_pairs={{0,2},{1,3},{2,0},{3,1},{4,6},{5,7},{6,4},{7,5},{8,10},{9,11},{10,... | collective-permute-start | bytes 786440 | tf_op jit(solution)/shard_map/ppermute | solution.py:677
  41.4 12.0 %copy-start.1 = (s32[8,16,2048]{2,1,0:T(8,128)S(1)}, s32[8,16,2048]{2,1,0:T(8,128)}, u32[]{:S(2)}) copy-start(s32[8,16,2048]{2,1,0:T(8,128)} %material.3) | copy-start | bytes 3145732
  41.4 12.0 %copy-start.2 = (f32[8,16,2048]{2,1,0:T(8,128)S(1)}, f32[8,16,2048]{2,1,0:T(8,128)}, u32[]{:S(2)}) copy-start(f32[8,16,2048]{2,1,0:T(8,128)} %history_old.1) | copy-start | bytes 3145732
  42.1 15.6 %collective-permute-start.19 = (f32[2,2,8,16,128]{4,3,2,1,0:T(8,128)S(1)}, f32[2,2,8,16,128]{4,3,2,1,0:T(8,128)S(1)}, u32[]{:S(2)}, u32[]{:S(2)}) collective-permute-start(f32[2,2,8,16,128]{4,3,2,1,0:T(8,128)S(1)} %get-tuple-element.116), channel_id=1, source_target_pairs={{0,1},{1,0},{2,3},{3,2},{4,5},{5,4},{6,7},{7,6},{8,9},{9,8},{10,11... | collective-permute-start | bytes 786440 | tf_op jit(solution)/shard_map/ppermute | solution.py:677
  44.6 11.7 %collective-permute-start.16 = (f32[3,8,2048]{2,1,0:T(8,128)S(1)}, f32[3,8,2048]{2,1,0:T(8,128)S(1)}, u32[]{:S(2)}, u32[]{:S(2)}) collective-permute-start(f32[3,8,2048]{2,1,0:T(8,128)S(1)} %get-tuple-element.102.y_low), channel_id=1, source_target_pairs={{1,0},{2,1},{3,2},{4,3},{5,4},{6,5},{7,6},{9,8},{10,9},{11,10},{12... | collective-permute-start | bytes 589832 | tf_op jit(solution)/shard_map/ppermute | solution.py:682
  45.9 10.5 %collective-permute-start.17 = (f32[3,8,2048]{2,1,0:T(8,128)S(1)}, f32[3,8,2048]{2,1,0:T(8,128)S(1)}, u32[]{:S(2)}, u32[]{:S(2)}) collective-permute-start(f32[3,8,2048]{2,1,0:T(8,128)S(1)} %get-tuple-element.100.x_low0), channel_id=1, source_target_pairs={{8,0},{16,8},{24,16},{9,1},{17,9},{25,17},{10,2},{18,10},{26,18},{... | collective-permute-start | bytes 589832 | tf_op jit(solution)/shard_map/ppermute | solution.py:682
  48.0 8.4 %collective-permute-start.18 = (f32[3,8,2048]{2,1,0:T(8,128)S(1)}, f32[3,8,2048]{2,1,0:T(8,128)S(1)}, u32[]{:S(2)}, u32[]{:S(2)}) collective-permute-start(f32[3,8,2048]{2,1,0:T(8,128)S(1)} %get-tuple-element.101.x_low1), channel_id=1, source_target_pairs={{8,0},{16,8},{24,16},{9,1},{17,9},{25,17},{10,2},{18,10},{26,18},{... | collective-permute-start | bytes 589832 | tf_op jit(solution)/shard_map/ppermute | solution.py:682
  56.4 1.3 %copy-start.3 = (s32[1,12]{1,0:T(1,128)S(1)}, s32[1,12]{1,0:T(1,128)}, u32[]{:S(2)}) copy-start(s32[1,12]{1,0:T(1,128)} %ids.1) | copy-start | bytes 148
  56.4 1.3 %copy-start.4 = (s32[1,12,1]{1,2,0:T(1,128)S(1)}, s32[1,12,1]{1,2,0:T(1,128)}, u32[]{:S(2)}) copy-start(s32[1,12,1]{1,2,0:T(1,128)} %param.14) | copy-start | bytes 148

commit v2 on v1

--- a/solution.py
+++ b/solution.py
@@ -128,11 +128,11 @@
         copy.start()
 
 
-def pack_planes(even, odd, read, nx, nt):
+def pack_planes(even, odd, read, nt, nx, components):
     def planes(low, high):
         for side, out in ((0, low), (nx - 1, high)):
             for t in range(nt):
-                for c in range(out[t].shape[0]):
+                for c in components:
                     value = read(c, side, t)
                     out[t][c, :, : value.shape[1]] = value
 
@@ -153,31 +153,34 @@
     ]
     fields = [pltpu.make_async_copy(field.at[c], u.at[c], sems.at[2, c]) for c in range(3)]
     owed = far_copies(tough, routes(lax.axis_size("yz"))[0], far_one, sems, 3)
+    start_all(fields)
     for pair in zip(*copies):
         start_all(pair)
-    start_all(fields + owed)
+    start_all(owed)
+    y_parity = lax.axis_index("yz") % 2
+    for copy in fields:
+        copy.wait()
+
+    def u_rows(low, high):
+        for side, out in ((0, low), (ny - 1, high)):
+            for x in range(nx):
+                for c in range(3):
+                    out[c, x : x + 1, :] = u[c, x, side : side + 1, :]
+
+    def stiff_rows(low, high):
+        for side, out in ((0, low), (ny - 1, high)):
+            for x in range(nx):
+                out[3, x : x + 1, :] = stiff[x, side : side + 1, :]
+
+    by_parity(y_parity, ye, yo, u_rows)
+    pack_planes((xe0, xe1), (xo0, xo1), lambda c, x, t: u[c, x, t * ROWS : (t + 1) * ROWS, :], nt, nx, range(3))
     for x in range(nx):
         copies[0][x].wait()
         copies[1][x].wait()
         d = 1.0 - damage_kept[x]
         stiff[x] = modulus(material_kept[x]) * (d * d + 0.001)
-    for copy in fields:
-        copy.wait()
-
-    def rows(low, high):
-        for side, out in ((0, low), (ny - 1, high)):
-            for x in range(nx):
-                for c in range(3):
-                    out[c, x : x + 1, :] = u[c, x, side : side + 1, :]
-                out[3, x : x + 1, :] = stiff[x, side : side + 1, :]
-
-    by_parity(lax.axis_index("yz") % 2, ye, yo, rows)
-
-    def read(c, x, t):
-        part = slice(t * ROWS, (t + 1) * ROWS)
-        return u[c, x, part, :] if c < 3 else stiff[x, part, :]
-
-    pack_planes((xe0, xe1), (xo0, xo1), read, nx, nt)
+    by_parity(y_parity, ye, yo, stiff_rows)
+    pack_planes((xe0, xe1), (xo0, xo1), lambda c, x, t: stiff[x, t * ROWS : (t + 1) * ROWS, :], nt, nx, (3,))
     for copy in owed:
         copy.wait()
 
@@ -313,8 +316,8 @@
 
 
 def face_one_kernel(
-    u, stiff, sye, syo, acc_x, acc_y, diag_x, diag_y, hxe0, hye, hyo, hxe1, hxo0, hxo1,
-    ye, yo, xe0, xe1, xo0, xo1, w_x, w_xy, s_x, w_y, w_yx, s_y, planes,
+    u, stiff, sye, syo, acc_x, acc_y, diag_x, diag_y, hxe0, hye, hyo, hxe1, hxo0, hxo1, hop_in,
+    ye, yo, xe0, xe1, xo0, xo1, w_x, w_xy, s_x, w_y, w_yx, s_y, planes, hop,
 ):
     _, nx, ny, nz = u.shape
     nt, nk = ny // ROWS, nz // LANES
@@ -379,7 +382,7 @@
     def read(c, x, t):
         return planes[LOW if x == 0 else HIGH, c, t * ROWS : (t + 1) * ROWS, :]
 
-    pack_planes((xe0, xe1), (xo0, xo1), read, nx, nt)
+    pack_planes((xe0, xe1), (xo0, xo1), read, nt, nx, range(3))
 
 
 def insert_faces(u, x_face, y_face):
@@ -471,9 +474,9 @@
 
 
 def energy_kernel(
-    u_in, x_low0, x_low1, y_low, x_high, y_high, material, history_old, tough_from, far_one, *rest
+    u_in, x_low0, x_low1, y_low, x_high, y_high, material, history_old, tough_from, damage_from, far_one, *rest
 ):
-    *fars, u, u_out, history, top, half_top, far, half_far, tough, rows, half_rows, sems = rest
+    *fars, u, u_out, history, top, half_top, far, half_far, tough, damage, rows, half_rows, sems = rest
     _, nx, ny, nz = u.shape
     nt, nk = ny // ROWS, nz // LANES
     x_low = (x_low0, x_low1)
@@ -488,7 +491,8 @@
     for d, arrived in zip(others, fars):
         sources.update({d: arrived.at[0], d ^ 1: arrived.at[1]})
     copies = [pltpu.make_async_copy(u.at[c], u_out.at[c], sems.at[c]) for c in range(3)]
-    copies += [pltpu.make_async_copy(source, tough.at[d], sems.at[3 + d]) for d, source in sources.items()]
+    copies += [pltpu.make_async_copy(source, tough.at[d], sems.at[4 + d]) for d, source in sources.items()]
+    copies.append(pltpu.make_async_copy(damage_from, damage, sems.at[3]))
     start_all(copies)
 
     def body(x, place):
@@ -532,13 +536,11 @@
 
 
 def history_kernel(
-    history_in, top, half_top, far, half_far, x_high, y_high, hy, hx0, hx1, damage_from, history, damage, energy, sems
+    history_in, top, half_top, far, half_far, x_high, y_high, hy, hx0, hx1, history, energy
 ):
-    nx, ny, nz = damage.shape
+    nx, ny, nz = history.shape
     nt, nk = ny // ROWS, nz // LANES
     hx = (hx0, hx1)
-    copy = pltpu.make_async_copy(damage_from, damage, sems.at[0])
-    copy.start()
 
     def squares(here, beyond):
         return sum([(beyond(c) - here(c)) ** 2 for c in range(3)])
@@ -561,20 +563,19 @@
             if t == nt - 1:
                 total = total + jnp.where(row_index() == ROWS - 1, moved(y_term, nx - 1, ROWS - 1), 0.0)
             put(history, (nx - 1,), t, k, jnp.maximum(tile(history, (nx - 1,), t, k), tile(half_far, (), t, k) * total))
-    copy.wait()
-
-
-def last_kernel(ids, owners, history, damage_in, tough_in, hop_two, damage, tough, history_out, damage_out, sems):
+
+
+def last_kernel(ids, owners, history, damage, tough, hop_two, history_out, damage_out, result, sems):
     nx, ny, nz = damage.shape
     nt = ny // ROWS
     count = ids.shape[1]
     me, size = lax.axis_index("yz"), lax.axis_size("yz")
-    fetched = [pltpu.make_async_copy(hop_two.at[i], tough.at[d ^ 1], sems.at[2 + i]) for i, d in enumerate((0, routes(size)[0]))]
-    start_all(fetched)
+    late = routes(size)[0] ^ 1
     saved = pltpu.make_async_copy(history, history_out, sems.at[0])
     saved.start()
-    for copy in fetched:
-        copy.wait()
+    rest = pltpu.make_async_copy(damage, damage_out, sems.at[1])
+    rest.start()
+    finished = []
     per = max(n for n in (1, 2, 3, 4, 6) if count % n == 0)
     cells = [(x, t) for x in range(nx) for t in range(nt)]
     i = lax.broadcasted_iota(jnp.int32, (2 * LANES, LANES), 0) % LANES
@@ -602,37 +603,42 @@
                 new[x, t] = first[x, t] + second[x, t] * total
         return new
 
-    def group(q, _):
+    def group(q):
         states = []
         for p in range(per):
             n = q * per + p
             owner = owners[0, n]
-            slot = lax.fori_loop(0, n, lambda m, found: found + (owners[0, m] == owner).astype(jnp.int32), jnp.int32(0))
+            slot = sum([(owners[0, m] == owner).astype(jnp.int32) for m in range(n)], jnp.int32(0))
             lanes = pl.ds(pl.multiple_of(ids[0, n] * LANES, LANES), LANES)
+            which = (owner ^ me == late).astype(jnp.int32)
+            by_hop = (owner ^ me == 1) | (owner ^ me == late)
             first, second, d = {}, {}, {}
             for x, t in cells:
                 part = slice(t * ROWS, (t + 1) * ROWS)
                 h2 = 2.0 * history[x, part, lanes]
                 g = tough[owner ^ me, slot, x, part, :]
+                g = jnp.where(by_hop, hop_two[which, slot, x, part, :], g)
                 g2 = g * LENGTH
                 inverse = 1.0 / (g / LENGTH + h2 + 6.0 * g2)
                 first[x, t] = h2 * inverse
                 second[x, t] = g2 * inverse
                 d[x, t] = damage[x, part, lanes]
-            states.append((lanes, first, second, d))
+            states.append((n, lanes, first, second, d))
         for _ in range(SWEEPS):
-            states = [(lanes, first, second, sweep(first, second, d)) for lanes, first, second, d in states]
-        for lanes, _, _, d in states:
+            states = [(n, lanes, first, second, sweep(first, second, d)) for n, lanes, first, second, d in states]
+        if q == 0:
+            rest.wait()
+        for n, lanes, _, _, d in states:
             for x, t in cells:
                 part = slice(t * ROWS, (t + 1) * ROWS)
-                damage[x, part, lanes] = jnp.maximum(d[x, t], damage[x, part, lanes])
-        return 0
-
-    lax.fori_loop(0, count // per, group, 0)
-    done = pltpu.make_async_copy(damage, damage_out, sems.at[1])
-    done.start()
-    saved.wait()
-    done.wait()
+                result[n, x, part, :] = jnp.maximum(d[x, t], damage[x, part, lanes])
+            finished.append(pltpu.make_async_copy(result.at[n], damage_out.at[:, :, lanes], sems.at[2 + n]))
+            finished[-1].start()
+
+    for q in range(count // per):
+        group(q)
+    for copy in [saved] + finished:
+        copy.wait()
 
 
 def even_pairs(axis):
@@ -742,12 +748,14 @@
         kept(u, stiff, force) + far_off(tough) + kept(brought[0], brought[3]),
         [pltpu.VMEM((2, 3, nx, ROWS, nz), F32), pltpu.VMEM((2, 1, nx, ROWS, nz), F32), copies(len(others))],
     )
+    *own, w_x, w_xy, s_x, w_y, w_yx, s_y, planes, hop = call(
+        face_one_kernel,
+        faces(3) + here(*[(2, ny, nz)] * 3, *[(2, nx, nz)] * 3, (2, 3, ny, nz), hop.shape),
+        kept(u, stiff, sent[0], sent[1], acc_x, acc_y, diag_x, diag_y, *brought, hop),
+        (),
+        {14: 13},
+    )
     hop = across(hop, 1)
-    *own, w_x, w_xy, s_x, w_y, w_yx, s_y, planes = call(
-        face_one_kernel,
-        faces(3) + here(*[(2, ny, nz)] * 3, *[(2, nx, nz)] * 3, (2, 3, ny, nz)),
-        kept(u, stiff, sent[0], sent[1], acc_x, acc_y, diag_x, diag_y, *brought),
-    )
     brought = exchange(*own)
     u1, u2, acc_x, acc_y, hop_two, *fars = call(
         inner_two_kernel,
@@ -768,26 +776,27 @@
     )
     hop_two = across(hop_two, 1)
     hy, hx0, hx1 = from_above(y_low, "yz"), from_above(x_low0, "gx"), from_above(x_low1, "gx")
-    _, new_displacement, history, *sums, tough_kept = call(
+    _, new_displacement, history, *sums, tough_kept, damage_kept = call(
         energy_kernel,
-        here(full) + [(full, HBM)] + here(cells, *[(nx, nz)] * 2, *[(ny, nz)] * 2, tough.shape),
-        kept(u2, x_low0, x_low1, y_low, x_high, y_high, material, history_old) + far_off(tough) + kept(far_one, *lasts),
-        [pltpu.VMEM((nx, ROWS, nz), F32), pltpu.VMEM((nx, ROWS, nz), F32), copies(3 + tough.shape[0])],
+        here(full) + [(full, HBM)] + here(cells, *[(nx, nz)] * 2, *[(ny, nz)] * 2, tough.shape, cells),
+        kept(u2, x_low0, x_low1, y_low, x_high, y_high, material, history_old) + far_off(tough, damage)
+        + kept(far_one, *lasts),
+        [pltpu.VMEM((nx, ROWS, nz), F32), pltpu.VMEM((nx, ROWS, nz), F32), copies(4 + tough.shape[0])],
         {0: 0},
     )
-    history, damage_kept = call(
+    (history,) = call(
         history_kernel,
-        here(cells, cells),
-        kept(history, *sums, x_high, y_high, hy, hx0, hx1) + far_off(damage),
-        [pltpu.VMEM((nx, nz), F32), copies(1)],
+        here(cells),
+        kept(history, *sums, x_high, y_high, hy, hx0, hx1),
+        [pltpu.VMEM((nx, nz), F32)],
         {0: 0},
     )
-    _, _, new_history, new_damage = call(
+    count = patch_ids.shape[1]
+    new_history, new_damage = call(
         last_kernel,
-        here(cells, tough.shape) + [(cells, HBM), (cells, HBM)],
+        [(cells, HBM), (cells, HBM)],
         [(patch_ids, pltpu.SMEM), (owners[:, :, 0], pltpu.SMEM)] + kept(history, damage_kept, tough_kept, hop_two),
-        [copies(4)],
-        {3: 0, 4: 1},
+        [pltpu.VMEM((count, nx, ny, LANES), F32), copies(2 + count)],
     )
     return (new_displacement, new_history, new_damage)
 

time: 63.9 us -> 62.1 us (0.972)
  the two profiles are of different devices: /device:TPU:0 before, /device:TPU:29 now
where the time goes in v2:
time: 62.1 us; the launch traced here: 61.9 us
  starting transfers between devices  33 us (53%)
  Pallas kernels  19.9 us (32%)
  waiting for transfers between devices  8.05 us (13%)
  between operations  0.86 us (1%)
    pallas_call x8, Pallas kernels, call(): pl.pallas_call(kernel, out_shape=shapes, in_specs=in_specs, out_specs=out...  19.9 us
    ppermute x3, starting transfers between devices, from_above(): return lax.ppermute(value, axis, [(i + 1, i) for i in range(size - 1)])  12.2 us
    ppermute x5, starting transfers between devices, across(): lax.ppermute(value, 'yz', [(i, i ^ d) for i in range(lax.axis_size('yz'))])  8.63 us
    ppermute x2, starting transfers between devices, exchange(): lax.ppermute(xe0, 'gx', even_pairs('gx'))  7.16 us
    ppermute x2, waiting for transfers between devices, exchange(): lax.ppermute(ye, 'yz', even_pairs('yz'))  4.34 us
    ppermute x2, starting transfers between devices, exchange(): lax.ppermute(xo1, both, odd_pairs('gx'))  2.69 us
    ppermute x3, waiting for transfers between devices, from_above(): return lax.ppermute(value, axis, [(i + 1, i) for i in range(size - 1)])  2.03 us
  transfers between devices with their start and end apart: 20, of which 5 were waited for; matrix products, arithmetic and copies ran while one was open for 0% of the time, Pallas kernels for 19%

profile of v2, /device:TPU:29, one launch (start us, length us, event | category | flops | bytes accessed | tf_op | source)
XLA Modules:
  0.0 61.9 jit_solution(3466343407399214546)
XLA Ops:
  0.6 3.0 %shard_map.103 = (f32[3,8,16,2048]{3,2,1,0:T(8,128)S(1)}, f32[8,16,2048]{2,1,0:T(8,128)S(1)}, f32[4,8,2048]{2,1,0:T(8,128)S(1)}, f32[4,8,2048]{2,1,0:T(8,128)S(1...) custom-call(f32[8,16,2048]{2,1,0:T(8,128)} %damage_from.1, ...), custom_call_target="tpu_custom_call" | custom-call | tf_op jit(solution)/shard_map/pallas_call | solution.py:699
  3.6 0.7 %collective-permute-start = (f32[4,8,2048]{2,1,0:T(8,128)S(1)}, f32[4,8,2048]{2,1,0:T(8,128)S(1)}, u32[]{:S(2)}, u32[]{:S(2)}) collective-permute-start(f32[4,8,2048]{2,1,0:T(8,128)S(1)} %get-tuple-element.63), channel_id=1, source_target_pairs={{0,8},{16,24},{8,0},{24,16},{1,9},{17,25},{9,1},{25,17},{2,10},{18... | collective-permute-start | bytes 786440 | tf_op jit(solution)/shard_map/ppermute | solution.py:668
  4.4 1.2 %collective-permute-start.4 = (f32[4,8,2176]{2,1,0:T(8,128)S(1)}, f32[4,8,2176]{2,1,0:T(8,128)S(1)}, u32[]{:S(2)}, u32[]{:S(2)}) collective-permute-start(f32[4,8,2176]{2,1,0:T(8,128)S(1)} %get-tuple-element.78), channel_id=1, source_target_pairs={{8,16},{9,17},{10,18},{11,19},{12,20},{13,21},{14,22},{15,23},{0,2... | collective-permute-start | bytes 835592 | tf_op jit(solution)/shard_map/ppermute | solution.py:672
  5.5 0.6 collective-permute-start.5
  6.1 0.4 collective-permute-start.1
  6.5 0.2 collective-permute-start.2
  6.7 0.4 collective-permute-start.3
  7.1 0.5 collective-permute-done.1.early1.hxe1
  7.6 1.4 %collective-permute-start.7 = (f32[2,2,8,16,128]{4,3,2,1,0:T(8,128)S(1)}, f32[2,2,8,16,128]{4,3,2,1,0:T(8,128)S(1)}, u32[]{:S(2)}, u32[]{:S(2)}) collective-permute-start(f32[2,2,8,16,128]{4,3,2,1,0:T(8,128)S(1)} %get-tuple-element.85), channel_id=1, source_target_pairs={{0,4},{1,5},{2,6},{3,7},{4,0},{5,1},{6,2},{7,3},{8,12},{9,13},{10,... | collective-permute-start | bytes 786440 | tf_op jit(solution)/shard_map/ppermute | solution.py:683
  9.0 3.9 %shard_map.104 = (f32[7,16,2048]{2,1,0:T(8,128)S(1)}, f32[8,16,2048]{2,1,0:T(8,128)S(1)}, f32[8,16,2048]{2,1,0:T(8,128)S(1)}, f32[8,16,2048]{2,1,0:T(8,128)S(1)}...) custom-call(f32[3,8,16,2048]{3,2,1,0:T(8,128)S(1)} %get-tuple-elemen, ...), custom_call_target="tpu_custom_call" | custom-call | tf_op jit(solution)/shard_map/pallas_call | solution.py:699
  12.9 1.5 %collective-permute-done.2.hye = f32[4,8,2048]{2,1,0:T(8,128)S(1)} collective-permute-done((f32[4,8,2048]{2,1,0:T(8,128)S(1)}, f32[4,8,2048]{2,1,0:T(8,128)S(1)}, u32[]{:S(2)}, u32[]{:S(2)}) %collective-permute-start.2) | collective-permute-done | bytes 262176 | tf_op jit(solution)/shard_map/ppermute | solution.py:669
  14.5 0.8 %shard_map.105 = (f32[3,8,2048]{2,1,0:T(8,128)S(1)}, f32[3,8,2048]{2,1,0:T(8,128)S(1)}, f32[3,8,2048]{2,1,0:T(8,128)S(1)}, f32[3,8,2048]{2,1,0:T(8,128)S(1)}, f3...) custom-call(f32[3,8,16,2048]{3,2,1,0:T(8,128)S(1)} %get-tuple-elemen, ...), custom_call_target="tpu_custom_call", output_to_operand_aliasing={{13}: (14, {})} | custom-call | tf_op jit(solution)/shard_map/pallas_call | solution.py:699
  15.2 3.4 %collective-permute-start.6 = (f32[2,2,8,16,128]{4,3,2,1,0:T(8,128)S(1)}, f32[2,2,8,16,128]{4,3,2,1,0:T(8,128)S(1)}, u32[]{:S(2)}, u32[]{:S(2)}) collective-permute-start(f32[2,2,8,16,128]{4,3,2,1,0:T(8,128)S(1)} %get-tuple-element.84), channel_id=1, source_target_pairs={{0,1},{1,0},{2,3},{3,2},{4,5},{5,4},{6,7},{7,6},{8,9},{9,8},{10,11... | collective-permute-start | bytes 786440 | tf_op jit(solution)/shard_map/ppermute | solution.py:683
  18.7 6.4 %collective-permute-start.8 = (f32[3,8,2048]{2,1,0:T(8,128)S(1)}, f32[3,8,2048]{2,1,0:T(8,128)S(1)}, u32[]{:S(2)}, u32[]{:S(2)}) collective-permute-start(f32[3,8,2048]{2,1,0:T(8,128)S(1)} %get-tuple-element.86), channel_id=1, source_target_pairs={{0,8},{16,24},{8,0},{24,16},{1,9},{17,25},{9,1},{25,17},{2,10},{18... | collective-permute-start | bytes 589832 | tf_op jit(solution)/shard_map/ppermute | solution.py:668
  25.1 0.0 collective-permute-start.12
  25.1 1.1 %collective-permute-done.7.far_one = f32[2,2,8,16,128]{4,3,2,1,0:T(8,128)S(1)} collective-permute-done((f32[2,2,8,16,128]{4,3,2,1,0:T(8,128)S(1)}, f32[2,2,8,16,128]{4,3,2,1,0:T(8,128)S(1)}, u32[]{:S(2)}, u32[]{:S(2)}) %collective-permute-start.7) | collective-permute-done | bytes 262176 | tf_op jit(solution)/shard_map/ppermute | solution.py:683
  26.3 2.1 %collective-permute-start.13 = (f32[3,8,2176]{2,1,0:T(8,128)S(1)}, f32[3,8,2176]{2,1,0:T(8,128)S(1)}, u32[]{:S(2)}, u32[]{:S(2)}) collective-permute-start(f32[3,8,2176]{2,1,0:T(8,128)S(1)} %get-tuple-element.99), channel_id=1, source_target_pairs={{8,16},{9,17},{10,18},{11,19},{12,20},{13,21},{14,22},{15,23},{0,2... | collective-permute-start | bytes 626696 | tf_op jit(solution)/shard_map/ppermute | solution.py:673
  28.4 0.1 collective-permute-start.11
  28.5 3.6 %shard_map.106 = (f32[3,8,16,2048]{3,2,1,0:T(8,128)S(1)}, f32[3,8,16,2048]{3,2,1,0:T(8,128)S(1)}, f32[2,3,16,2048]{3,2,1,0:T(8,128)S(1)}, f32[2,3,8,2048]{3,2,1,...) custom-call(f32[3,8,16,2048]{3,2,1,0:T(8,128)S(1)} %get-tuple-elemen, ...), custom_call_target="tpu_custom_call", output_to_operand_aliasing={{0}: (0, {})} | custom-call | tf_op jit(solution)/shard_map/pallas_call | solution.py:699
  32.1 1.6 %collective-permute-start.14 = (f32[2,2,8,16,128]{4,3,2,1,0:T(8,128)S(1)}, f32[2,2,8,16,128]{4,3,2,1,0:T(8,128)S(1)}, u32[]{:S(2)}, u32[]{:S(2)}) collective-permute-start(f32[2,2,8,16,128]{4,3,2,1,0:T(8,128)S(1)} %get-tuple-element.106), channel_id=1, source_target_pairs={{0,6},{1,7},{2,4},{3,5},{4,2},{5,3},{6,0},{7,1},{8,14},{9,15},{10,... | collective-permute-start | bytes 786440 | tf_op jit(solution)/shard_map/ppermute | solution.py:683
  33.7 2.8 %collective-permute-done.10.hye = f32[3,8,2048]{2,1,0:T(8,128)S(1)} collective-permute-done((f32[3,8,2048]{2,1,0:T(8,128)S(1)}, f32[3,8,2048]{2,1,0:T(8,128)S(1)}, u32[]{:S(2)}, u32[]{:S(2)}) %collective-permute-start.10) | collective-permute-done | bytes 196640 | tf_op jit(solution)/shard_map/ppermute | solution.py:669
  36.5 0.0 copy-start.1
  36.6 0.6 shard_map.107
  37.1 2.3 %collective-permute-start.19 = (f32[2,2,8,16,128]{4,3,2,1,0:T(8,128)S(1)}, f32[2,2,8,16,128]{4,3,2,1,0:T(8,128)S(1)}, u32[]{:S(2)}, u32[]{:S(2)}) collective-permute-start(f32[2,2,8,16,128]{4,3,2,1,0:T(8,128)S(1)} %get-tuple-element.116), channel_id=1, source_target_pairs={{0,1},{1,0},{2,3},{3,2},{4,5},{5,4},{6,7},{7,6},{8,9},{9,8},{10,11... | collective-permute-start | bytes 786440 | tf_op jit(solution)/shard_map/ppermute | solution.py:683
  39.4 1.9 %collective-permute-start.16 = (f32[3,8,2048]{2,1,0:T(8,128)S(1)}, f32[3,8,2048]{2,1,0:T(8,128)S(1)}, u32[]{:S(2)}, u32[]{:S(2)}) collective-permute-start(f32[3,8,2048]{2,1,0:T(8,128)S(1)} %get-tuple-element.103.y_low), channel_id=1, source_target_pairs={{1,0},{2,1},{3,2},{4,3},{5,4},{6,5},{7,6},{9,8},{10,9},{11,10},{12... | collective-permute-start | bytes 589832 | tf_op jit(solution)/shard_map/ppermute | solution.py:688
  41.3 8.4 %collective-permute-start.17 = (f32[3,8,2048]{2,1,0:T(8,128)S(1)}, f32[3,8,2048]{2,1,0:T(8,128)S(1)}, u32[]{:S(2)}, u32[]{:S(2)}) collective-permute-start(f32[3,8,2048]{2,1,0:T(8,128)S(1)} %get-tuple-element.101.x_low0), channel_id=1, source_target_pairs={{8,0},{16,8},{24,16},{9,1},{17,9},{25,17},{10,2},{18,10},{26,18},{... | collective-permute-start | bytes 589832 | tf_op jit(solution)/shard_map/ppermute | solution.py:688
  49.8 1.9 %collective-permute-start.18 = (f32[3,8,2048]{2,1,0:T(8,128)S(1)}, f32[3,8,2048]{2,1,0:T(8,128)S(1)}, u32[]{:S(2)}, u32[]{:S(2)}) collective-permute-start(f32[3,8,2048]{2,1,0:T(8,128)S(1)} %get-tuple-element.102.x_low1), channel_id=1, source_target_pairs={{8,0},{16,8},{24,16},{9,1},{17,9},{25,17},{10,2},{18,10},{26,18},{... | collective-permute-start | bytes 589832 | tf_op jit(solution)/shard_map/ppermute | solution.py:688
  51.7 2.9 %shard_map.108 = (f32[3,8,16,2048]{3,2,1,0:T(8,128)S(1)}, f32[3,8,16,2048]{3,2,1,0:T(8,128)}, f32[8,16,2048]{2,1,0:T(8,128)S(1)}, f32[8,2048]{1,0:T(8,128)S(1)},...) custom-call(f32[3,8,16,2048]{3,2,1,0:T(8,128)S(1)} %get-tuple-elemen, ...), custom_call_target="tpu_custom_call", output_to_operand_aliasing={{0}: (0, {})} | custom-call | tf_op jit(solution)/shard_map/pallas_call | solution.py:699
  54.7 0.0 copy-start.3
  54.7 2.0 %collective-permute-done.18.hx1 = f32[3,8,2048]{2,1,0:T(8,128)S(1)} collective-permute-done((f32[3,8,2048]{2,1,0:T(8,128)S(1)}, f32[3,8,2048]{2,1,0:T(8,128)S(1)}, u32[]{:S(2)}, u32[]{:S(2)}) %collective-permute-start.18) | collective-permute-done | bytes 196640 | tf_op jit(solution)/shard_map/ppermute | solution.py:688
  56.8 0.2 shard_map.109.history
  57.0 4.9 %shard_map.110 = (f32[8,16,2048]{2,1,0:T(8,128)}, f32[8,16,2048]{2,1,0:T(8,128)}) custom-call(s32[1,12]{1,0:T(1,128)S(1)} %copy-done.3, s32[1,12]{1,0:T(1,128)S(1)} %bitcast.2, f32[8,16,2048]{2,1,0:T(8,128)S(1)} %shard_map.109.history, f32[8,16,2048]{2,1,0:T(8,128)S(1)} %get-tuple-element.114.damage, f32[8,2,8,16,128]{4,3,2,1,0:T(8,128)S(1)} %get-tuple-element.115.tough, ...), custom_call_target="tpu_custom_call" | custom-call | tf_op jit(solution)/shard_map/pallas_call | solution.py:699
  (26 shorter events, 0.1 us)
Async XLA Ops:
  0.6 8.4 %copy-start = (f32[3,8,16,2048]{3,2,1,0:T(8,128)S(1)}, f32[3,8,16,2048]{3,2,1,0:T(8,128)}, u32[]{:S(2)}) copy-start(f32[3,8,16,2048]{3,2,1,0:T(8,128)} %force.3) | copy-start | bytes 9437188
  3.6 3.1 %collective-permute-start = (f32[4,8,2048]{2,1,0:T(8,128)S(1)}, f32[4,8,2048]{2,1,0:T(8,128)S(1)}, u32[]{:S(2)}, u32[]{:S(2)}) collective-permute-start(f32[4,8,2048]{2,1,0:T(8,128)S(1)} %get-tuple-element.63), channel_id=1, source_target_pairs={{0,8},{16,24},{8,0},{24,16},{1,9},{17,25},{9,1},{25,17},{2,10},{18... | collective-permute-start | bytes 786440 | tf_op jit(solution)/shard_map/ppermute | solution.py:668
  4.4 10.1 %collective-permute-start.4 = (f32[4,8,2176]{2,1,0:T(8,128)S(1)}, f32[4,8,2176]{2,1,0:T(8,128)S(1)}, u32[]{:S(2)}, u32[]{:S(2)}) collective-permute-start(f32[4,8,2176]{2,1,0:T(8,128)S(1)} %get-tuple-element.78), channel_id=1, source_target_pairs={{8,16},{9,17},{10,18},{11,19},{12,20},{13,21},{14,22},{15,23},{0,2... | collective-permute-start | bytes 835592 | tf_op jit(solution)/shard_map/ppermute | solution.py:672
  5.5 8.9 %collective-permute-start.5 = (f32[4,8,2176]{2,1,0:T(8,128)S(1)}, f32[4,8,2176]{2,1,0:T(8,128)S(1)}, u32[]{:S(2)}, u32[]{:S(2)}) collective-permute-start(f32[4,8,2176]{2,1,0:T(8,128)S(1)} %get-tuple-element.79), channel_id=1, source_target_pairs={{8,16},{9,17},{10,18},{11,19},{12,20},{13,21},{14,22},{15,23},{0,2... | collective-permute-start | bytes 835592 | tf_op jit(solution)/shard_map/ppermute | solution.py:673
  6.1 1.5 %collective-permute-start.1 = (f32[4,8,2048]{2,1,0:T(8,128)S(1)}, f32[4,8,2048]{2,1,0:T(8,128)S(1)}, u32[]{:S(2)}, u32[]{:S(2)}) collective-permute-start(f32[4,8,2048]{2,1,0:T(8,128)S(1)} %get-tuple-element.64), channel_id=1, source_target_pairs={{0,8},{16,24},{8,0},{24,16},{1,9},{17,25},{9,1},{25,17},{2,10},{18... | collective-permute-start | bytes 786440 | tf_op jit(solution)/shard_map/ppermute | solution.py:671
  6.5 8.0 %collective-permute-start.2 = (f32[4,8,2048]{2,1,0:T(8,128)S(1)}, f32[4,8,2048]{2,1,0:T(8,128)S(1)}, u32[]{:S(2)}, u32[]{:S(2)}) collective-permute-start(f32[4,8,2048]{2,1,0:T(8,128)S(1)} %get-tuple-element.72.sye), channel_id=1, source_target_pairs={{0,1},{2,3},{4,5},{6,7},{1,0},{3,2},{5,4},{7,6},{8,9},{10,11},{12,... | collective-permute-start | bytes 786440 | tf_op jit(solution)/shard_map/ppermute | solution.py:669
  6.7 7.8 %collective-permute-start.3 = (f32[4,8,2048]{2,1,0:T(8,128)S(1)}, f32[4,8,2048]{2,1,0:T(8,128)S(1)}, u32[]{:S(2)}, u32[]{:S(2)}) collective-permute-start(f32[4,8,2048]{2,1,0:T(8,128)S(1)} %get-tuple-element.73.syo), channel_id=1, source_target_pairs={{1,2},{9,10},{17,18},{25,26},{3,4},{11,12},{19,20},{27,28},{5,6},{... | collective-permute-start | bytes 786440 | tf_op jit(solution)/shard_map/ppermute | solution.py:670
  7.6 18.6 %collective-permute-start.7 = (f32[2,2,8,16,128]{4,3,2,1,0:T(8,128)S(1)}, f32[2,2,8,16,128]{4,3,2,1,0:T(8,128)S(1)}, u32[]{:S(2)}, u32[]{:S(2)}) collective-permute-start(f32[2,2,8,16,128]{4,3,2,1,0:T(8,128)S(1)} %get-tuple-element.85), channel_id=1, source_target_pairs={{0,4},{1,5},{2,6},{3,7},{4,0},{5,1},{6,2},{7,3},{8,12},{9,13},{10,... | collective-permute-start | bytes 786440 | tf_op jit(solution)/shard_map/ppermute | solution.py:683
  15.2 13.2 %collective-permute-start.6 = (f32[2,2,8,16,128]{4,3,2,1,0:T(8,128)S(1)}, f32[2,2,8,16,128]{4,3,2,1,0:T(8,128)S(1)}, u32[]{:S(2)}, u32[]{:S(2)}) collective-permute-start(f32[2,2,8,16,128]{4,3,2,1,0:T(8,128)S(1)} %get-tuple-element.84), channel_id=1, source_target_pairs={{0,1},{1,0},{2,3},{3,2},{4,5},{5,4},{6,7},{7,6},{8,9},{9,8},{10,11... | collective-permute-start | bytes 786440 | tf_op jit(solution)/shard_map/ppermute | solution.py:683
  18.7 9.7 %collective-permute-start.8 = (f32[3,8,2048]{2,1,0:T(8,128)S(1)}, f32[3,8,2048]{2,1,0:T(8,128)S(1)}, u32[]{:S(2)}, u32[]{:S(2)}) collective-permute-start(f32[3,8,2048]{2,1,0:T(8,128)S(1)} %get-tuple-element.86), channel_id=1, source_target_pairs={{0,8},{16,24},{8,0},{24,16},{1,9},{17,25},{9,1},{25,17},{2,10},{18... | collective-permute-start | bytes 589832 | tf_op jit(solution)/shard_map/ppermute | solution.py:668
  25.1 3.3 %collective-permute-start.9 = (f32[3,8,2048]{2,1,0:T(8,128)S(1)}, f32[3,8,2048]{2,1,0:T(8,128)S(1)}, u32[]{:S(2)}, u32[]{:S(2)}) collective-permute-start(f32[3,8,2048]{2,1,0:T(8,128)S(1)} %get-tuple-element.87), channel_id=1, source_target_pairs={{0,8},{16,24},{8,0},{24,16},{1,9},{17,25},{9,1},{25,17},{2,10},{18... | collective-permute-start | bytes 589832 | tf_op jit(solution)/shard_map/ppermute | solution.py:671
  25.1 11.4 %collective-permute-start.12 = (f32[3,8,2176]{2,1,0:T(8,128)S(1)}, f32[3,8,2176]{2,1,0:T(8,128)S(1)}, u32[]{:S(2)}, u32[]{:S(2)}) collective-permute-start(f32[3,8,2176]{2,1,0:T(8,128)S(1)} %get-tuple-element.98), channel_id=1, source_target_pairs={{8,16},{9,17},{10,18},{11,19},{12,20},{13,21},{14,22},{15,23},{0,2... | collective-permute-start | bytes 626696 | tf_op jit(solution)/shard_map/ppermute | solution.py:672
  26.3 10.3 %collective-permute-start.13 = (f32[3,8,2176]{2,1,0:T(8,128)S(1)}, f32[3,8,2176]{2,1,0:T(8,128)S(1)}, u32[]{:S(2)}, u32[]{:S(2)}) collective-permute-start(f32[3,8,2176]{2,1,0:T(8,128)S(1)} %get-tuple-element.99), channel_id=1, source_target_pairs={{8,16},{9,17},{10,18},{11,19},{12,20},{13,21},{14,22},{15,23},{0,2... | collective-permute-start | bytes 626696 | tf_op jit(solution)/shard_map/ppermute | solution.py:673
  28.4 8.1 %collective-permute-start.10 = (f32[3,8,2048]{2,1,0:T(8,128)S(1)}, f32[3,8,2048]{2,1,0:T(8,128)S(1)}, u32[]{:S(2)}, u32[]{:S(2)}) collective-permute-start(f32[3,8,2048]{2,1,0:T(8,128)S(1)} %get-tuple-element.81.sye), channel_id=1, source_target_pairs={{0,1},{2,3},{4,5},{6,7},{1,0},{3,2},{5,4},{7,6},{8,9},{10,11},{12,... | collective-permute-start | bytes 589832 | tf_op jit(solution)/shard_map/ppermute | solution.py:669
  28.4 8.1 %collective-permute-start.11 = (f32[3,8,2048]{2,1,0:T(8,128)S(1)}, f32[3,8,2048]{2,1,0:T(8,128)S(1)}, u32[]{:S(2)}, u32[]{:S(2)}) collective-permute-start(f32[3,8,2048]{2,1,0:T(8,128)S(1)} %get-tuple-element.82.syo), channel_id=1, source_target_pairs={{1,2},{9,10},{17,18},{25,26},{3,4},{11,12},{19,20},{27,28},{5,6},{... | collective-permute-start | bytes 589832 | tf_op jit(solution)/shard_map/ppermute | solution.py:670
  32.1 17.6 %collective-permute-start.14 = (f32[2,2,8,16,128]{4,3,2,1,0:T(8,128)S(1)}, f32[2,2,8,16,128]{4,3,2,1,0:T(8,128)S(1)}, u32[]{:S(2)}, u32[]{:S(2)}) collective-permute-start(f32[2,2,8,16,128]{4,3,2,1,0:T(8,128)S(1)} %get-tuple-element.106), channel_id=1, source_target_pairs={{0,6},{1,7},{2,4},{3,5},{4,2},{5,3},{6,0},{7,1},{8,14},{9,15},{10,... | collective-permute-start | bytes 786440 | tf_op jit(solution)/shard_map/ppermute | solution.py:683
  36.5 15.2 %collective-permute-start.15 = (f32[2,2,8,16,128]{4,3,2,1,0:T(8,128)S(1)}, f32[2,2,8,16,128]{4,3,2,1,0:T(8,128)S(1)}, u32[]{:S(2)}, u32[]{:S(2)}) collective-permute-start(f32[2,2,8,16,128]{4,3,2,1,0:T(8,128)S(1)} %get-tuple-element.107), channel_id=1, source_target_pairs={{0,2},{1,3},{2,0},{3,1},{4,6},{5,7},{6,4},{7,5},{8,10},{9,11},{10,... | collective-permute-start | bytes 786440 | tf_op jit(solution)/shard_map/ppermute | solution.py:683
  36.5 15.2 %copy-start.1 = (s32[8,16,2048]{2,1,0:T(8,128)S(1)}, s32[8,16,2048]{2,1,0:T(8,128)}, u32[]{:S(2)}) copy-start(s32[8,16,2048]{2,1,0:T(8,128)} %material.3) | copy-start | bytes 3145732
  36.5 15.2 %copy-start.2 = (f32[8,16,2048]{2,1,0:T(8,128)S(1)}, f32[8,16,2048]{2,1,0:T(8,128)}, u32[]{:S(2)}) copy-start(f32[8,16,2048]{2,1,0:T(8,128)} %history_old.1) | copy-start | bytes 3145732
  37.1 19.8 %collective-permute-start.19 = (f32[2,2,8,16,128]{4,3,2,1,0:T(8,128)S(1)}, f32[2,2,8,16,128]{4,3,2,1,0:T(8,128)S(1)}, u32[]{:S(2)}, u32[]{:S(2)}) collective-permute-start(f32[2,2,8,16,128]{4,3,2,1,0:T(8,128)S(1)} %get-tuple-element.116), channel_id=1, source_target_pairs={{0,1},{1,0},{2,3},{3,2},{4,5},{5,4},{6,7},{7,6},{8,9},{9,8},{10,11... | collective-permute-start | bytes 786440 | tf_op jit(solution)/shard_map/ppermute | solution.py:683
  39.4 15.3 %collective-permute-start.16 = (f32[3,8,2048]{2,1,0:T(8,128)S(1)}, f32[3,8,2048]{2,1,0:T(8,128)S(1)}, u32[]{:S(2)}, u32[]{:S(2)}) collective-permute-start(f32[3,8,2048]{2,1,0:T(8,128)S(1)} %get-tuple-element.103.y_low), channel_id=1, source_target_pairs={{1,0},{2,1},{3,2},{4,3},{5,4},{6,5},{7,6},{9,8},{10,9},{11,10},{12... | collective-permute-start | bytes 589832 | tf_op jit(solution)/shard_map/ppermute | solution.py:688
  41.3 13.4 %collective-permute-start.17 = (f32[3,8,2048]{2,1,0:T(8,128)S(1)}, f32[3,8,2048]{2,1,0:T(8,128)S(1)}, u32[]{:S(2)}, u32[]{:S(2)}) collective-permute-start(f32[3,8,2048]{2,1,0:T(8,128)S(1)} %get-tuple-element.101.x_low0), channel_id=1, source_target_pairs={{8,0},{16,8},{24,16},{9,1},{17,9},{25,17},{10,2},{18,10},{26,18},{... | collective-permute-start | bytes 589832 | tf_op jit(solution)/shard_map/ppermute | solution.py:688
  49.8 7.0 %collective-permute-start.18 = (f32[3,8,2048]{2,1,0:T(8,128)S(1)}, f32[3,8,2048]{2,1,0:T(8,128)S(1)}, u32[]{:S(2)}, u32[]{:S(2)}) collective-permute-start(f32[3,8,2048]{2,1,0:T(8,128)S(1)} %get-tuple-element.102.x_low1), channel_id=1, source_target_pairs={{8,0},{16,8},{24,16},{9,1},{17,9},{25,17},{10,2},{18,10},{26,18},{... | collective-permute-start | bytes 589832 | tf_op jit(solution)/shard_map/ppermute | solution.py:688
  54.7 2.3 %copy-start.3 = (s32[1,12]{1,0:T(1,128)S(1)}, s32[1,12]{1,0:T(1,128)}, u32[]{:S(2)}) copy-start(s32[1,12]{1,0:T(1,128)} %ids.1) | copy-start | bytes 148
  54.7 2.3 %copy-start.4 = (s32[1,12,1]{1,2,0:T(1,128)S(1)}, s32[1,12,1]{1,2,0:T(1,128)}, u32[]{:S(2)}) copy-start(s32[1,12,1]{1,2,0:T(1,128)} %param.14) | copy-start | bytes 148

commit v3 on v2

--- a/solution.py
+++ b/solution.py
@@ -407,24 +407,28 @@
 
 
 def inner_two_kernel(
-    u_in, scale, force, wx, wya, wyb, wza, wzb, sye, syo, planes, tough, hop, far_one, early0, early1,
+    u_in, scale, force, wx, wya, wyb, wza, wzb, sye, syo, planes, tough, far_one, early0, early1,
     u, out, acc_x, acc_y, hop_two, *rest,
 ):
     *fars, faces, sems = rest
     me = lax.axis_index("yz")
     copies = [
-        pltpu.make_async_copy(tough.at[me ^ 1], hop_two.at[0], sems.at[2 * len(fars)]),
-        pltpu.make_async_copy(far_one.at[1], hop_two.at[1], sems.at[2 * len(fars) + 1]),
+        pltpu.make_async_copy(tough.at[me ^ 1], hop_two.at[0], sems.at[len(fars)]),
+        pltpu.make_async_copy(far_one.at[1], hop_two.at[1], sems.at[len(fars) + 1]),
     ]
     for i, (d, far) in enumerate(zip(routes(lax.axis_size("yz"))[1], fars)):
-        copies.append(pltpu.make_async_copy(tough.at[me ^ d], far.at[0], sems.at[2 * i]))
-        copies.append(pltpu.make_async_copy(hop.at[i], far.at[1], sems.at[2 * i + 1]))
+        copies.append(pltpu.make_async_copy(tough.at[me ^ d], far.at[0], sems.at[i]))
     start_all(copies)
     hy = lax.axis_index("yz") % 2
     insert_faces(u, lambda side, c, t, k: tile(planes, (side, c), t, k), lambda side, c, k: own_side(hy, side, sye, syo, (c,), k))
     inner_pass(u, force, wx, wya, wyb, wza, wzb, scale, out, acc_x, acc_y, faces)
     for copy in copies:
         copy.wait()
+
+
+def forward_kernel(hop, *rest):
+    for i, far in enumerate(rest[len(rest) // 2 :]):
+        far[1] = hop[i]
 
 
 def face_two_kernel(
@@ -724,8 +728,8 @@
     assert nx == ROWS and ny == 2 * ROWS
     full, cells, halves = (3, nx, ny, nz), (nx, ny, nz), (3, ROWS, nz)
 
-    def faces(count):
-        return here(*[(count, nx, nz)] * 2, *[(count, ROWS, nz)] * 2, *[(count, ROWS, nz + LANES)] * 2)
+    def faces(count, extra):
+        return here(*[(count, nx, nz)] * 2, *[(count, ROWS, nz)] * 2, *[(count, ROWS, nz + extra)] * 2)
 
     def copies(count):
         return pltpu.SemaphoreType.DMA((count,))
@@ -735,7 +739,7 @@
     first, others = routes(lax.axis_size("yz"))
     u, stiff, *sent, far_one = call(
         begin_kernel,
-        here(full, cells) + faces(4) + here(pair),
+        here(full, cells) + faces(4, LANES) + here(pair),
         far_off(damage, material, displacement, tough),
         [pltpu.VMEM(cells, F32), pltpu.VMEM(cells, jnp.int32), pltpu.SemaphoreType.DMA((4, nx))],
     )
@@ -750,7 +754,7 @@
     )
     *own, w_x, w_xy, s_x, w_y, w_yx, s_y, planes, hop = call(
         face_one_kernel,
-        faces(3) + here(*[(2, ny, nz)] * 3, *[(2, nx, nz)] * 3, (2, 3, ny, nz), hop.shape),
+        faces(3, 0) + here(*[(2, ny, nz)] * 3, *[(2, nx, nz)] * 3, (2, 3, ny, nz), hop.shape),
         kept(u, stiff, sent[0], sent[1], acc_x, acc_y, diag_x, diag_y, *brought, hop),
         (),
         {14: 13},
@@ -762,14 +766,15 @@
         here(full, full, (2, 3, ny, nz), (2, 3, nx, nz), pair, *[pair for _ in others]),
         kept(u1, scale, force, wx, wya, wyb, wza, wzb, own[0], own[1], planes)
         + far_off(tough)
-        + kept(hop, far_one, brought[0], brought[3]),
-        [pltpu.VMEM((2, 3, nx, ROWS, nz), F32), copies(2 + 2 * len(others))],
+        + kept(far_one, brought[0], brought[3]),
+        [pltpu.VMEM((2, 3, nx, ROWS, nz), F32), copies(2 + len(others))],
         {0: 0},
     )
+    fars = call(forward_kernel, here(*[pair for _ in others]), kept(hop, *fars), (), {1 + i: i for i in range(len(others))})
     lasts = [across(value, d) for d, value in zip(others, fars)]
     x_low0, x_low1, y_low, x_high, y_high, hop_two = call(
         face_two_kernel,
-        here(halves, halves, (3, nx, nz), (3, ny, nz), (3, nx, nz), hop_two.shape),
+        here(halves, halves, (3, nx, nz + LANES), (3, ny, nz), (3, nx, nz), hop_two.shape),
         kept(u1, own[0], own[1], acc_x, acc_y, w_x, w_xy, s_x, w_y, w_yx, s_y, *brought, hop_two),
         (),
         {17: 5},

time: 62.1 us -> 62.3 us (level)
  starting transfers between devices: 33 us -> 34.4 us
  waiting for transfers between devices: 8.05 us -> 7.32 us
    ppermute x5, starting transfers between devices: 8.63 us -> 9.74 us  [across(): lax.ppermute(value, 'yz', [(i, i ^ d) for i in range(lax.axis_size('yz'))])]
    ppermute x2, waiting for transfers between devices: 4.34 us -> 3.59 us  [exchange(): lax.ppermute(ye, 'yz', even_pairs('yz'))]
    pallas_call x8 -> x9, Pallas kernels: 19.9 us -> 19.5 us  [call(): pl.pallas_call(kernel, out_shape=shapes, in_specs=in_specs, out_specs=out...]
where the time goes in v3:
time: 62.3 us; the launch traced here: 62 us
  starting transfers between devices  34.4 us (55%)
  Pallas kernels  19.5 us (31%)
  waiting for transfers between devices  7.32 us (12%)
  between operations  0.84 us (1%)
    pallas_call x9, Pallas kernels, call(): pl.pallas_call(kernel, out_shape=shapes, in_specs=in_specs, out_specs=out...  19.5 us
    ppermute x3, starting transfers between devices, from_above(): return lax.ppermute(value, axis, [(i + 1, i) for i in range(size - 1)])  12.5 us
    ppermute x5, starting transfers between devices, across(): lax.ppermute(value, 'yz', [(i, i ^ d) for i in range(lax.axis_size('yz'))])  9.74 us
    ppermute x2, starting transfers between devices, exchange(): lax.ppermute(xe0, 'gx', even_pairs('gx'))  7.16 us
    ppermute x2, waiting for transfers between devices, exchange(): lax.ppermute(ye, 'yz', even_pairs('yz'))  3.59 us
    ppermute x2, starting transfers between devices, exchange(): lax.ppermute(xo1, both, odd_pairs('gx'))  2.69 us
    ppermute x3, waiting for transfers between devices, from_above(): return lax.ppermute(value, axis, [(i + 1, i) for i in range(size - 1)])  2.05 us
  transfers between devices with their start and end apart: 20, of which 5 were waited for; matrix products, arithmetic and copies ran while one was open for 0% of the time, Pallas kernels for 19%

profile of v3, /device:TPU:29, one launch (start us, length us, event | category | flops | bytes accessed | tf_op | source)
XLA Modules:
  0.0 62.0 jit_solution(2366836320957087735)
XLA Ops:
  0.6 3.0 %shard_map.103 = (f32[3,8,16,2048]{3,2,1,0:T(8,128)S(1)}, f32[8,16,2048]{2,1,0:T(8,128)S(1)}, f32[4,8,2048]{2,1,0:T(8,128)S(1)}, f32[4,8,2048]{2,1,0:T(8,128)S(1...) custom-call(f32[8,16,2048]{2,1,0:T(8,128)} %damage_from.1, ...), custom_call_target="tpu_custom_call" | custom-call | tf_op jit(solution)/shard_map/pallas_call | solution.py:703
  3.6 0.7 %collective-permute-start = (f32[4,8,2048]{2,1,0:T(8,128)S(1)}, f32[4,8,2048]{2,1,0:T(8,128)S(1)}, u32[]{:S(2)}, u32[]{:S(2)}) collective-permute-start(f32[4,8,2048]{2,1,0:T(8,128)S(1)} %get-tuple-element.65), channel_id=1, source_target_pairs={{0,8},{16,24},{8,0},{24,16},{1,9},{17,25},{9,1},{25,17},{2,10},{18... | collective-permute-start | bytes 786440 | tf_op jit(solution)/shard_map/ppermute | solution.py:672
  4.4 1.2 %collective-permute-start.4 = (f32[4,8,2176]{2,1,0:T(8,128)S(1)}, f32[4,8,2176]{2,1,0:T(8,128)S(1)}, u32[]{:S(2)}, u32[]{:S(2)}) collective-permute-start(f32[4,8,2176]{2,1,0:T(8,128)S(1)} %get-tuple-element.80), channel_id=1, source_target_pairs={{8,16},{9,17},{10,18},{11,19},{12,20},{13,21},{14,22},{15,23},{0,2... | collective-permute-start | bytes 835592 | tf_op jit(solution)/shard_map/ppermute | solution.py:676
  5.5 0.6 collective-permute-start.5
  6.1 0.4 collective-permute-start.1
  6.5 0.2 collective-permute-start.2
  6.7 0.4 collective-permute-start.3
  7.1 0.5 collective-permute-done.1.early1.hxe1
  7.6 1.4 %collective-permute-start.6 = (f32[2,2,8,16,128]{4,3,2,1,0:T(8,128)S(1)}, f32[2,2,8,16,128]{4,3,2,1,0:T(8,128)S(1)}, u32[]{:S(2)}, u32[]{:S(2)}) collective-permute-start(f32[2,2,8,16,128]{4,3,2,1,0:T(8,128)S(1)} %get-tuple-element.86), channel_id=1, source_target_pairs={{0,4},{1,5},{2,6},{3,7},{4,0},{5,1},{6,2},{7,3},{8,12},{9,13},{10,... | collective-permute-start | bytes 786440 | tf_op jit(solution)/shard_map/ppermute | solution.py:687
  9.0 3.9 %shard_map.104 = (f32[7,16,2048]{2,1,0:T(8,128)S(1)}, f32[8,16,2048]{2,1,0:T(8,128)S(1)}, f32[8,16,2048]{2,1,0:T(8,128)S(1)}, f32[8,16,2048]{2,1,0:T(8,128)S(1)}...) custom-call(f32[3,8,16,2048]{3,2,1,0:T(8,128)S(1)} %get-tuple-elemen, ...), custom_call_target="tpu_custom_call" | custom-call | tf_op jit(solution)/shard_map/pallas_call | solution.py:703
  12.9 1.6 %collective-permute-done.2.hye = f32[4,8,2048]{2,1,0:T(8,128)S(1)} collective-permute-done((f32[4,8,2048]{2,1,0:T(8,128)S(1)}, f32[4,8,2048]{2,1,0:T(8,128)S(1)}, u32[]{:S(2)}, u32[]{:S(2)}) %collective-permute-start.2) | collective-permute-done | bytes 262176 | tf_op jit(solution)/shard_map/ppermute | solution.py:673
  14.5 0.8 %shard_map.105 = (f32[3,8,2048]{2,1,0:T(8,128)S(1)}, f32[3,8,2048]{2,1,0:T(8,128)S(1)}, f32[3,8,2048]{2,1,0:T(8,128)S(1)}, f32[3,8,2048]{2,1,0:T(8,128)S(1)}, f3...) custom-call(f32[3,8,16,2048]{3,2,1,0:T(8,128)S(1)} %get-tuple-elemen, ...), custom_call_target="tpu_custom_call", output_to_operand_aliasing={{13}: (14, {})} | custom-call | tf_op jit(solution)/shard_map/pallas_call | solution.py:703
  15.2 3.4 %collective-permute-start.13 = (f32[2,2,8,16,128]{4,3,2,1,0:T(8,128)S(1)}, f32[2,2,8,16,128]{4,3,2,1,0:T(8,128)S(1)}, u32[]{:S(2)}, u32[]{:S(2)}) collective-permute-start(f32[2,2,8,16,128]{4,3,2,1,0:T(8,128)S(1)} %get-tuple-element.107), channel_id=1, source_target_pairs={{0,1},{1,0},{2,3},{3,2},{4,5},{5,4},{6,7},{7,6},{8,9},{9,8},{10,11... | collective-permute-start | bytes 786440 | tf_op jit(solution)/shard_map/ppermute | solution.py:687
  18.7 6.4 %collective-permute-start.7 = (f32[3,8,2048]{2,1,0:T(8,128)S(1)}, f32[3,8,2048]{2,1,0:T(8,128)S(1)}, u32[]{:S(2)}, u32[]{:S(2)}) collective-permute-start(f32[3,8,2048]{2,1,0:T(8,128)S(1)} %get-tuple-element.87), channel_id=1, source_target_pairs={{0,8},{16,24},{8,0},{24,16},{1,9},{17,25},{9,1},{25,17},{2,10},{18... | collective-permute-start | bytes 589832 | tf_op jit(solution)/shard_map/ppermute | solution.py:672
  25.1 0.0 collective-permute-start.11
  25.1 1.1 %collective-permute-done.6.far_one = f32[2,2,8,16,128]{4,3,2,1,0:T(8,128)S(1)} collective-permute-done((f32[2,2,8,16,128]{4,3,2,1,0:T(8,128)S(1)}, f32[2,2,8,16,128]{4,3,2,1,0:T(8,128)S(1)}, u32[]{:S(2)}, u32[]{:S(2)}) %collective-permute-start.6) | collective-permute-done | bytes 262176 | tf_op jit(solution)/shard_map/ppermute | solution.py:687
  26.3 2.1 %collective-permute-start.12 = (f32[3,8,2048]{2,1,0:T(8,128)S(1)}, f32[3,8,2048]{2,1,0:T(8,128)S(1)}, u32[]{:S(2)}, u32[]{:S(2)}) collective-permute-start(f32[3,8,2048]{2,1,0:T(8,128)S(1)} %get-tuple-element.100), channel_id=1, source_target_pairs={{8,16},{9,17},{10,18},{11,19},{12,20},{13,21},{14,22},{15,23},{0,2... | collective-permute-start | bytes 589832 | tf_op jit(solution)/shard_map/ppermute | solution.py:677
  28.4 0.1 collective-permute-start.10
  28.5 3.2 %shard_map.106 = (f32[3,8,16,2048]{3,2,1,0:T(8,128)S(1)}, f32[3,8,16,2048]{3,2,1,0:T(8,128)S(1)}, f32[2,3,16,2048]{3,2,1,0:T(8,128)S(1)}, f32[2,3,8,2048]{3,2,1,...) custom-call(f32[3,8,16,2048]{3,2,1,0:T(8,128)S(1)} %get-tuple-elemen, ...), custom_call_target="tpu_custom_call", output_to_operand_aliasing={{0}: (0, {})} | custom-call | tf_op jit(solution)/shard_map/pallas_call | solution.py:703
  31.7 1.6 %collective-permute-start.14 = (f32[2,2,8,16,128]{4,3,2,1,0:T(8,128)S(1)}, f32[2,2,8,16,128]{4,3,2,1,0:T(8,128)S(1)}, u32[]{:S(2)}, u32[]{:S(2)}) collective-permute-start(f32[2,2,8,16,128]{4,3,2,1,0:T(8,128)S(1)} %get-tuple-element.110), channel_id=1, source_target_pairs={{0,6},{1,7},{2,4},{3,5},{4,2},{5,3},{6,0},{7,1},{8,14},{9,15},{10,... | collective-permute-start | bytes 786440 | tf_op jit(solution)/shard_map/ppermute | solution.py:687
  33.3 1.1 %collective-permute-start.15 = (f32[2,2,8,16,128]{4,3,2,1,0:T(8,128)S(1)}, f32[2,2,8,16,128]{4,3,2,1,0:T(8,128)S(1)}, u32[]{:S(2)}, u32[]{:S(2)}) collective-permute-start(f32[2,2,8,16,128]{4,3,2,1,0:T(8,128)S(1)} %get-tuple-element.111), channel_id=1, source_target_pairs={{0,2},{1,3},{2,0},{3,1},{4,6},{5,7},{6,4},{7,5},{8,10},{9,11},{10,... | collective-permute-start | bytes 786440 | tf_op jit(solution)/shard_map/ppermute | solution.py:687
  34.4 2.0 %collective-permute-done.9.hye = f32[3,8,2048]{2,1,0:T(8,128)S(1)} collective-permute-done((f32[3,8,2048]{2,1,0:T(8,128)S(1)}, f32[3,8,2048]{2,1,0:T(8,128)S(1)}, u32[]{:S(2)}, u32[]{:S(2)}) %collective-permute-start.9) | collective-permute-done | bytes 196640 | tf_op jit(solution)/shard_map/ppermute | solution.py:673
  36.4 0.6 shard_map.107
  37.0 2.3 %collective-permute-start.19 = (f32[2,2,8,16,128]{4,3,2,1,0:T(8,128)S(1)}, f32[2,2,8,16,128]{4,3,2,1,0:T(8,128)S(1)}, u32[]{:S(2)}, u32[]{:S(2)}) collective-permute-start(f32[2,2,8,16,128]{4,3,2,1,0:T(8,128)S(1)} %get-tuple-element.120), channel_id=1, source_target_pairs={{0,1},{1,0},{2,3},{3,2},{4,5},{5,4},{6,7},{7,6},{8,9},{9,8},{10,11... | collective-permute-start | bytes 786440 | tf_op jit(solution)/shard_map/ppermute | solution.py:687
  39.3 1.9 %collective-permute-start.16 = (f32[3,8,2176]{2,1,0:T(8,128)S(1)}, f32[3,8,2176]{2,1,0:T(8,128)S(1)}, u32[]{:S(2)}, u32[]{:S(2)}) collective-permute-start(f32[3,8,2176]{2,1,0:T(8,128)S(1)} %get-tuple-element.104.y_low), channel_id=1, source_target_pairs={{1,0},{2,1},{3,2},{4,3},{5,4},{6,5},{7,6},{9,8},{10,9},{11,10},{12... | collective-permute-start | bytes 626696 | tf_op jit(solution)/shard_map/ppermute | solution.py:692
  41.2 8.6 %collective-permute-start.17 = (f32[3,8,2048]{2,1,0:T(8,128)S(1)}, f32[3,8,2048]{2,1,0:T(8,128)S(1)}, u32[]{:S(2)}, u32[]{:S(2)}) collective-permute-start(f32[3,8,2048]{2,1,0:T(8,128)S(1)} %get-tuple-element.102.x_low0), channel_id=1, source_target_pairs={{8,0},{16,8},{24,16},{9,1},{17,9},{25,17},{10,2},{18,10},{26,18},{... | collective-permute-start | bytes 589832 | tf_op jit(solution)/shard_map/ppermute | solution.py:692
  49.9 1.9 %collective-permute-start.18 = (f32[3,8,2048]{2,1,0:T(8,128)S(1)}, f32[3,8,2048]{2,1,0:T(8,128)S(1)}, u32[]{:S(2)}, u32[]{:S(2)}) collective-permute-start(f32[3,8,2048]{2,1,0:T(8,128)S(1)} %get-tuple-element.103.x_low1), channel_id=1, source_target_pairs={{8,0},{16,8},{24,16},{9,1},{17,9},{25,17},{10,2},{18,10},{26,18},{... | collective-permute-start | bytes 589832 | tf_op jit(solution)/shard_map/ppermute | solution.py:692
  51.8 2.9 %shard_map.109 = (f32[3,8,16,2048]{3,2,1,0:T(8,128)S(1)}, f32[3,8,16,2048]{3,2,1,0:T(8,128)}, f32[8,16,2048]{2,1,0:T(8,128)S(1)}, f32[8,2048]{1,0:T(8,128)S(1)},...) custom-call(f32[3,8,16,2048]{3,2,1,0:T(8,128)S(1)} %get-tuple-elemen, ...), custom_call_target="tpu_custom_call", output_to_operand_aliasing={{0}: (0, {})} | custom-call | tf_op jit(solution)/shard_map/pallas_call | solution.py:703
  54.8 0.0 copy-start.4
  54.8 2.0 %collective-permute-done.18.hx1 = f32[3,8,2048]{2,1,0:T(8,128)S(1)} collective-permute-done((f32[3,8,2048]{2,1,0:T(8,128)S(1)}, f32[3,8,2048]{2,1,0:T(8,128)S(1)}, u32[]{:S(2)}, u32[]{:S(2)}) %collective-permute-start.18) | collective-permute-done | bytes 196640 | tf_op jit(solution)/shard_map/ppermute | solution.py:692
  56.9 0.2 shard_map.110.history
  57.1 4.9 %shard_map.111 = (f32[8,16,2048]{2,1,0:T(8,128)}, f32[8,16,2048]{2,1,0:T(8,128)}) custom-call(s32[1,12]{1,0:T(1,128)S(1)} %copy-done.3, s32[1,12]{1,0:T(1,128)S(1)} %bitcast.2, f32[8,16,2048]{2,1,0:T(8,128)S(1)} %shard_map.110.history, f32[8,16,2048]{2,1,0:T(8,128)S(1)} %get-tuple-element.118.damage, f32[8,2,8,16,128]{4,3,2,1,0:T(8,128)S(1)} %get-tuple-element.119.tough, ...), custom_call_target="tpu_custom_call" | custom-call | tf_op jit(solution)/shard_map/pallas_call | solution.py:703
  (27 shorter events, 0.1 us)
Async XLA Ops:
  0.6 8.4 %copy-start = (f32[3,8,16,2048]{3,2,1,0:T(8,128)S(1)}, f32[3,8,16,2048]{3,2,1,0:T(8,128)}, u32[]{:S(2)}) copy-start(f32[3,8,16,2048]{3,2,1,0:T(8,128)} %force.3) | copy-start | bytes 9437188
  3.6 3.1 %collective-permute-start = (f32[4,8,2048]{2,1,0:T(8,128)S(1)}, f32[4,8,2048]{2,1,0:T(8,128)S(1)}, u32[]{:S(2)}, u32[]{:S(2)}) collective-permute-start(f32[4,8,2048]{2,1,0:T(8,128)S(1)} %get-tuple-element.65), channel_id=1, source_target_pairs={{0,8},{16,24},{8,0},{24,16},{1,9},{17,25},{9,1},{25,17},{2,10},{18... | collective-permute-start | bytes 786440 | tf_op jit(solution)/shard_map/ppermute | solution.py:672
  4.4 10.1 %collective-permute-start.4 = (f32[4,8,2176]{2,1,0:T(8,128)S(1)}, f32[4,8,2176]{2,1,0:T(8,128)S(1)}, u32[]{:S(2)}, u32[]{:S(2)}) collective-permute-start(f32[4,8,2176]{2,1,0:T(8,128)S(1)} %get-tuple-element.80), channel_id=1, source_target_pairs={{8,16},{9,17},{10,18},{11,19},{12,20},{13,21},{14,22},{15,23},{0,2... | collective-permute-start | bytes 835592 | tf_op jit(solution)/shard_map/ppermute | solution.py:676
  5.5 8.9 %collective-permute-start.5 = (f32[4,8,2176]{2,1,0:T(8,128)S(1)}, f32[4,8,2176]{2,1,0:T(8,128)S(1)}, u32[]{:S(2)}, u32[]{:S(2)}) collective-permute-start(f32[4,8,2176]{2,1,0:T(8,128)S(1)} %get-tuple-element.81), channel_id=1, source_target_pairs={{8,16},{9,17},{10,18},{11,19},{12,20},{13,21},{14,22},{15,23},{0,2... | collective-permute-start | bytes 835592 | tf_op jit(solution)/shard_map/ppermute | solution.py:677
  6.1 1.5 %collective-permute-start.1 = (f32[4,8,2048]{2,1,0:T(8,128)S(1)}, f32[4,8,2048]{2,1,0:T(8,128)S(1)}, u32[]{:S(2)}, u32[]{:S(2)}) collective-permute-start(f32[4,8,2048]{2,1,0:T(8,128)S(1)} %get-tuple-element.66), channel_id=1, source_target_pairs={{0,8},{16,24},{8,0},{24,16},{1,9},{17,25},{9,1},{25,17},{2,10},{18... | collective-permute-start | bytes 786440 | tf_op jit(solution)/shard_map/ppermute | solution.py:675
  6.5 8.0 %collective-permute-start.2 = (f32[4,8,2048]{2,1,0:T(8,128)S(1)}, f32[4,8,2048]{2,1,0:T(8,128)S(1)}, u32[]{:S(2)}, u32[]{:S(2)}) collective-permute-start(f32[4,8,2048]{2,1,0:T(8,128)S(1)} %get-tuple-element.74.sye), channel_id=1, source_target_pairs={{0,1},{2,3},{4,5},{6,7},{1,0},{3,2},{5,4},{7,6},{8,9},{10,11},{12,... | collective-permute-start | bytes 786440 | tf_op jit(solution)/shard_map/ppermute | solution.py:673
  6.7 7.8 %collective-permute-start.3 = (f32[4,8,2048]{2,1,0:T(8,128)S(1)}, f32[4,8,2048]{2,1,0:T(8,128)S(1)}, u32[]{:S(2)}, u32[]{:S(2)}) collective-permute-start(f32[4,8,2048]{2,1,0:T(8,128)S(1)} %get-tuple-element.75.syo), channel_id=1, source_target_pairs={{1,2},{9,10},{17,18},{25,26},{3,4},{11,12},{19,20},{27,28},{5,6},{... | collective-permute-start | bytes 786440 | tf_op jit(solution)/shard_map/ppermute | solution.py:674
  7.6 18.6 %collective-permute-start.6 = (f32[2,2,8,16,128]{4,3,2,1,0:T(8,128)S(1)}, f32[2,2,8,16,128]{4,3,2,1,0:T(8,128)S(1)}, u32[]{:S(2)}, u32[]{:S(2)}) collective-permute-start(f32[2,2,8,16,128]{4,3,2,1,0:T(8,128)S(1)} %get-tuple-element.86), channel_id=1, source_target_pairs={{0,4},{1,5},{2,6},{3,7},{4,0},{5,1},{6,2},{7,3},{8,12},{9,13},{10,... | collective-permute-start | bytes 786440 | tf_op jit(solution)/shard_map/ppermute | solution.py:687
  15.2 16.4 %collective-permute-start.13 = (f32[2,2,8,16,128]{4,3,2,1,0:T(8,128)S(1)}, f32[2,2,8,16,128]{4,3,2,1,0:T(8,128)S(1)}, u32[]{:S(2)}, u32[]{:S(2)}) collective-permute-start(f32[2,2,8,16,128]{4,3,2,1,0:T(8,128)S(1)} %get-tuple-element.107), channel_id=1, source_target_pairs={{0,1},{1,0},{2,3},{3,2},{4,5},{5,4},{6,7},{7,6},{8,9},{9,8},{10,11... | collective-permute-start | bytes 786440 | tf_op jit(solution)/shard_map/ppermute | solution.py:687
  18.7 9.7 %collective-permute-start.7 = (f32[3,8,2048]{2,1,0:T(8,128)S(1)}, f32[3,8,2048]{2,1,0:T(8,128)S(1)}, u32[]{:S(2)}, u32[]{:S(2)}) collective-permute-start(f32[3,8,2048]{2,1,0:T(8,128)S(1)} %get-tuple-element.87), channel_id=1, source_target_pairs={{0,8},{16,24},{8,0},{24,16},{1,9},{17,25},{9,1},{25,17},{2,10},{18... | collective-permute-start | bytes 589832 | tf_op jit(solution)/shard_map/ppermute | solution.py:672
  25.1 3.3 %collective-permute-start.8 = (f32[3,8,2048]{2,1,0:T(8,128)S(1)}, f32[3,8,2048]{2,1,0:T(8,128)S(1)}, u32[]{:S(2)}, u32[]{:S(2)}) collective-permute-start(f32[3,8,2048]{2,1,0:T(8,128)S(1)} %get-tuple-element.88), channel_id=1, source_target_pairs={{0,8},{16,24},{8,0},{24,16},{1,9},{17,25},{9,1},{25,17},{2,10},{18... | collective-permute-start | bytes 589832 | tf_op jit(solution)/shard_map/ppermute | solution.py:675
  25.1 8.2 %collective-permute-start.11 = (f32[3,8,2048]{2,1,0:T(8,128)S(1)}, f32[3,8,2048]{2,1,0:T(8,128)S(1)}, u32[]{:S(2)}, u32[]{:S(2)}) collective-permute-start(f32[3,8,2048]{2,1,0:T(8,128)S(1)} %get-tuple-element.99), channel_id=1, source_target_pairs={{8,16},{9,17},{10,18},{11,19},{12,20},{13,21},{14,22},{15,23},{0,2... | collective-permute-start | bytes 589832 | tf_op jit(solution)/shard_map/ppermute | solution.py:676
  26.3 8.1 %collective-permute-start.12 = (f32[3,8,2048]{2,1,0:T(8,128)S(1)}, f32[3,8,2048]{2,1,0:T(8,128)S(1)}, u32[]{:S(2)}, u32[]{:S(2)}) collective-permute-start(f32[3,8,2048]{2,1,0:T(8,128)S(1)} %get-tuple-element.100), channel_id=1, source_target_pairs={{8,16},{9,17},{10,18},{11,19},{12,20},{13,21},{14,22},{15,23},{0,2... | collective-permute-start | bytes 589832 | tf_op jit(solution)/shard_map/ppermute | solution.py:677
  28.4 8.1 %collective-permute-start.9 = (f32[3,8,2048]{2,1,0:T(8,128)S(1)}, f32[3,8,2048]{2,1,0:T(8,128)S(1)}, u32[]{:S(2)}, u32[]{:S(2)}) collective-permute-start(f32[3,8,2048]{2,1,0:T(8,128)S(1)} %get-tuple-element.83.sye), channel_id=1, source_target_pairs={{0,1},{2,3},{4,5},{6,7},{1,0},{3,2},{5,4},{7,6},{8,9},{10,11},{12,... | collective-permute-start | bytes 589832 | tf_op jit(solution)/shard_map/ppermute | solution.py:673
  28.4 8.1 %collective-permute-start.10 = (f32[3,8,2048]{2,1,0:T(8,128)S(1)}, f32[3,8,2048]{2,1,0:T(8,128)S(1)}, u32[]{:S(2)}, u32[]{:S(2)}) collective-permute-start(f32[3,8,2048]{2,1,0:T(8,128)S(1)} %get-tuple-element.84.syo), channel_id=1, source_target_pairs={{1,2},{9,10},{17,18},{25,26},{3,4},{11,12},{19,20},{27,28},{5,6},{... | collective-permute-start | bytes 589832 | tf_op jit(solution)/shard_map/ppermute | solution.py:674
  31.7 18.1 %collective-permute-start.14 = (f32[2,2,8,16,128]{4,3,2,1,0:T(8,128)S(1)}, f32[2,2,8,16,128]{4,3,2,1,0:T(8,128)S(1)}, u32[]{:S(2)}, u32[]{:S(2)}) collective-permute-start(f32[2,2,8,16,128]{4,3,2,1,0:T(8,128)S(1)} %get-tuple-element.110), channel_id=1, source_target_pairs={{0,6},{1,7},{2,4},{3,5},{4,2},{5,3},{6,0},{7,1},{8,14},{9,15},{10,... | collective-permute-start | bytes 786440 | tf_op jit(solution)/shard_map/ppermute | solution.py:687
  33.3 18.5 %collective-permute-start.15 = (f32[2,2,8,16,128]{4,3,2,1,0:T(8,128)S(1)}, f32[2,2,8,16,128]{4,3,2,1,0:T(8,128)S(1)}, u32[]{:S(2)}, u32[]{:S(2)}) collective-permute-start(f32[2,2,8,16,128]{4,3,2,1,0:T(8,128)S(1)} %get-tuple-element.111), channel_id=1, source_target_pairs={{0,2},{1,3},{2,0},{3,1},{4,6},{5,7},{6,4},{7,5},{8,10},{9,11},{10,... | collective-permute-start | bytes 786440 | tf_op jit(solution)/shard_map/ppermute | solution.py:687
  36.4 15.4 %copy-start.1 = (s32[8,16,2048]{2,1,0:T(8,128)S(1)}, s32[8,16,2048]{2,1,0:T(8,128)}, u32[]{:S(2)}) copy-start(s32[8,16,2048]{2,1,0:T(8,128)} %material.3) | copy-start | bytes 3145732
  36.4 15.4 %copy-start.2 = (f32[8,16,2048]{2,1,0:T(8,128)S(1)}, f32[8,16,2048]{2,1,0:T(8,128)}, u32[]{:S(2)}) copy-start(f32[8,16,2048]{2,1,0:T(8,128)} %history_old.1) | copy-start | bytes 3145732
  37.0 20.1 %collective-permute-start.19 = (f32[2,2,8,16,128]{4,3,2,1,0:T(8,128)S(1)}, f32[2,2,8,16,128]{4,3,2,1,0:T(8,128)S(1)}, u32[]{:S(2)}, u32[]{:S(2)}) collective-permute-start(f32[2,2,8,16,128]{4,3,2,1,0:T(8,128)S(1)} %get-tuple-element.120), channel_id=1, source_target_pairs={{0,1},{1,0},{2,3},{3,2},{4,5},{5,4},{6,7},{7,6},{8,9},{9,8},{10,11... | collective-permute-start | bytes 786440 | tf_op jit(solution)/shard_map/ppermute | solution.py:687
  39.3 17.6 %collective-permute-start.16 = (f32[3,8,2176]{2,1,0:T(8,128)S(1)}, f32[3,8,2176]{2,1,0:T(8,128)S(1)}, u32[]{:S(2)}, u32[]{:S(2)}) collective-permute-start(f32[3,8,2176]{2,1,0:T(8,128)S(1)} %get-tuple-element.104.y_low), channel_id=1, source_target_pairs={{1,0},{2,1},{3,2},{4,3},{5,4},{6,5},{7,6},{9,8},{10,9},{11,10},{12... | collective-permute-start | bytes 626696 | tf_op jit(solution)/shard_map/ppermute | solution.py:692
  41.2 13.6 %collective-permute-start.17 = (f32[3,8,2048]{2,1,0:T(8,128)S(1)}, f32[3,8,2048]{2,1,0:T(8,128)S(1)}, u32[]{:S(2)}, u32[]{:S(2)}) collective-permute-start(f32[3,8,2048]{2,1,0:T(8,128)S(1)} %get-tuple-element.102.x_low0), channel_id=1, source_target_pairs={{8,0},{16,8},{24,16},{9,1},{17,9},{25,17},{10,2},{18,10},{26,18},{... | collective-permute-start | bytes 589832 | tf_op jit(solution)/shard_map/ppermute | solution.py:692
  49.9 7.0 %collective-permute-start.18 = (f32[3,8,2048]{2,1,0:T(8,128)S(1)}, f32[3,8,2048]{2,1,0:T(8,128)S(1)}, u32[]{:S(2)}, u32[]{:S(2)}) collective-permute-start(f32[3,8,2048]{2,1,0:T(8,128)S(1)} %get-tuple-element.103.x_low1), channel_id=1, source_target_pairs={{8,0},{16,8},{24,16},{9,1},{17,9},{25,17},{10,2},{18,10},{26,18},{... | collective-permute-start | bytes 589832 | tf_op jit(solution)/shard_map/ppermute | solution.py:692
  54.8 2.3 %copy-start.3 = (s32[1,12]{1,0:T(1,128)S(1)}, s32[1,12]{1,0:T(1,128)}, u32[]{:S(2)}) copy-start(s32[1,12]{1,0:T(1,128)} %ids.1) | copy-start | bytes 148
  54.8 2.3 %copy-start.4 = (s32[1,12,1]{1,2,0:T(1,128)S(1)}, s32[1,12,1]{1,2,0:T(1,128)}, u32[]{:S(2)}) copy-start(s32[1,12,1]{1,2,0:T(1,128)} %param.14) | copy-start | bytes 148
